TPU v7x, 32 devices: a whole 2x2x4 slice. The times are simulated.
32 devices in a mesh: dp: 4 (over z), seq: 2 (over y), tensor: 4 (over x, core).
Axes of the slice: x: 2, y: 2, z: 4, core: 2. Of those that a mesh axis runs over, the one named last changes fastest.
Arguments:
- tokens: bfloat16 [8, 1024, 1152], P('dp', 'seq'), may hold values from -6 to 6
- positions: int32 [8, 1024], P('dp', 'seq'), may hold values from 0 to 2046, as said below
- out_grad: bfloat16 [8, 1024, 1152], P('dp', 'seq'), may hold values from -6 to 6
- q_weight: bfloat16 [1152, 1024], P(('dp', 'seq'), 'tensor'), may hold values from -0.1875 to 0.1875
- kv_weight: bfloat16 [1152, 512], P(('dp', 'seq', 'tensor')), may hold values from -0.1875 to 0.1875
- o_weight: bfloat16 [1024, 1152], P('tensor', ('dp', 'seq')), may hold values from -0.1875 to 0.1875
- gate_weight: bfloat16 [1152, 6912], P(('dp', 'seq'), 'tensor'), may hold values from -0.1875 to 0.1875
- up_weight: bfloat16 [1152, 6912], P(('dp', 'seq'), 'tensor'), may hold values from -0.1875 to 0.1875
- down_weight: bfloat16 [6912, 1152], P('tensor', ('dp', 'seq')), may hold values from -0.078125 to 0.078125
- attn_in_gain: bfloat16 [1152], P(('dp', 'seq', 'tensor')), may hold values from -0.5 to 0.5
- attn_out_gain: bfloat16 [1152], P(('dp', 'seq', 'tensor')), may hold values from -0.5 to 0.5
- ffn_in_gain: bfloat16 [1152], P(('dp', 'seq', 'tensor')), may hold values from -0.5 to 0.5
- ffn_out_gain: bfloat16 [1152], P(('dp', 'seq', 'tensor')), may hold values from -0.5 to 0.5
- q_gain: bfloat16 [256], P(('dp', 'seq', 'tensor')), may hold values from -0.5 to 0.5
- k_gain: bfloat16 [256], P(('dp', 'seq', 'tensor')), may hold values from -0.5 to 0.5
Outputs:
- result: bfloat16 [8, 1024, 1152], P('dp', 'seq')
- input_grad: bfloat16 [8, 1024, 1152], P('dp', 'seq')
- q_weight_grad: float32 [1152, 1024], P(('dp', 'seq'), 'tensor')
- kv_weight_grad: float32 [1152, 512], P(('dp', 'seq', 'tensor'))
- o_weight_grad: float32 [1024, 1152], P('tensor', ('dp', 'seq'))
- gate_weight_grad: float32 [1152, 6912], P(('dp', 'seq'), 'tensor')
- up_weight_grad: float32 [1152, 6912], P(('dp', 'seq'), 'tensor')
- down_weight_grad: float32 [6912, 1152], P('tensor', ('dp', 'seq'))
- attn_in_gain_grad: float32 [1152], P(('dp', 'seq', 'tensor'))
- attn_out_gain_grad: float32 [1152], P(('dp', 'seq', 'tensor'))
- ffn_in_gain_grad: float32 [1152], P(('dp', 'seq', 'tensor'))
- ffn_out_gain_grad: float32 [1152], P(('dp', 'seq', 'tensor'))
- q_gain_grad: float32 [256], P(('dp', 'seq', 'tensor'))
- k_gain_grad: float32 [256], P(('dp', 'seq', 'tensor'))
Inputs may be any that keep to these rules, and one draw needn't show every extreme that they name: `positions`: in every sequence the token of index i has position 2 i or 2 i - 1; the first token has 0 and the last 2 (1023).
All inputs are finite; a program needn't handle non-finite values.
Results may differ from a plain program's by a relative error of at most 0.025.
Values may be sent and summed in bfloat16 or wider, within the bound.
A program may use at most 192 MiB of HBM per device.

v0:
```python
import jax
import jax.numpy as jnp
from jax import lax
from jax.sharding import PartitionSpec as P

D = 1152
HEAD = 256
MICRO = 2


EPS = 1e-06
QSCALE = 0.0625
MASKED = -1e30


def angles(positions, width_n):
    half_w = width_n // 2
    freq_t = 1000000.0 ** (-(jnp.arange(half_w, dtype=jnp.float32) * 2.0 / width_n))
    turn_t = positions.astype(jnp.float32)[..., None] * freq_t
    turn_t = jnp.concatenate([turn_t, turn_t], axis=-1)
    return (jnp.cos(turn_t), jnp.sin(turn_t))


def normalize(values):
    factor = lax.rsqrt(jnp.mean(values * values, axis=-1, keepdims=True) + EPS)
    return (values * factor, factor)


def norm_back(scaled, factor, upstream):
    return factor * (upstream - scaled * jnp.mean(upstream * scaled, axis=-1, keepdims=True))


def rotate(values, cos_t, sin_t):
    half_w = values.shape[-1] // 2
    turned = jnp.concatenate([-values[..., half_w:], values[..., :half_w]], axis=-1)
    return values * cos_t + turned * sin_t


def rotate_back(grad_in, cos_t, sin_t):
    half_w = grad_in.shape[-1] // 2
    moved_up = grad_in * sin_t
    turned = jnp.concatenate([moved_up[..., half_w:], -moved_up[..., :half_w]], axis=-1)
    return grad_in * cos_t + turned


def product(pattern, left_m, right_m):
    return jnp.einsum(pattern, left_m, right_m, preferred_element_type=jnp.float32)


def gelu_mix(gate_v, upper_v):
    return jax.nn.gelu(gate_v, approximate=True) * upper_v


def all_rows(values):
    return jnp.sum(values.reshape(-1, values.shape[-1]), axis=0)


def my_rows(values):
    flat_v = values.reshape(-1, values.shape[-1])
    share_n = flat_v.shape[0] // lax.axis_size("tensor")
    return lax.dynamic_slice_in_dim(flat_v, lax.axis_index("tensor") * share_n, share_n, 0)


def share_sum(values):
    return jnp.sum(my_rows(values), axis=0)


def sum_tensor(values):
    return lax.psum(values, "tensor")


def fetch_front(matrices, small_set):
    gathered = (
        lax.all_gather(matrices[0], ("dp", "seq"), axis=0, tiled=True),
        lax.all_gather(matrices[1], ("dp", "seq"), axis=1, tiled=True),
        lax.all_gather(matrices[2], ("dp", "seq"), axis=0, tiled=True),
        lax.all_gather(matrices[3], ("dp", "seq"), axis=0, tiled=True),
        lax.all_gather(matrices[4], ("dp", "seq"), axis=1, tiled=True),
    )
    shared = (
        lax.all_gather(small_set[0], ("dp", "seq", "tensor"), axis=0, tiled=True),
        lax.all_gather(small_set[1], ("dp", "seq", "tensor"), axis=0, tiled=True),
        lax.all_gather(small_set[2], ("dp", "seq", "tensor"), axis=0, tiled=True),
        lax.all_gather(small_set[3], ("dp", "seq", "tensor"), axis=0, tiled=True),
        lax.all_gather(small_set[4], ("dp", "seq", "tensor"), axis=0, tiled=True),
        lax.all_gather(small_set[5], ("dp", "seq", "tensor"), axis=0, tiled=True),
        lax.all_gather(small_set[6], ("dp", "seq", "tensor"), axis=0, tiled=True),
    )
    return (gathered, shared)


def fetch_back(matrices, small_set):
    gathered = (
        lax.all_gather(matrices[0], ("dp", "seq"), axis=0, tiled=True),
        lax.all_gather(matrices[1], ("dp", "seq"), axis=1, tiled=True),
        lax.all_gather(matrices[2], ("dp", "seq"), axis=0, tiled=True),
        lax.all_gather(matrices[3], ("dp", "seq"), axis=0, tiled=True),
        lax.all_gather(matrices[4], ("dp", "seq"), axis=1, tiled=True),
    )
    shared = (
        lax.all_gather(small_set[0], ("dp", "seq", "tensor"), axis=0, tiled=True),
        lax.all_gather(small_set[1], ("dp", "seq", "tensor"), axis=0, tiled=True),
        lax.all_gather(small_set[2], ("dp", "seq", "tensor"), axis=0, tiled=True),
        lax.all_gather(small_set[3], ("dp", "seq", "tensor"), axis=0, tiled=True),
        lax.all_gather(small_set[4], ("dp", "seq", "tensor"), axis=0, tiled=True),
        lax.all_gather(small_set[5], ("dp", "seq", "tensor"), axis=0, tiled=True),
        lax.all_gather(small_set[6], ("dp", "seq", "tensor"), axis=0, tiled=True),
    )
    return (gathered, shared)


def unpack(weight_set):
    gathered, shared = weight_set
    scales = tuple((1.0 + entry.astype(jnp.float32) for entry in shared[1:]))
    return (gathered, shared[0], scales)


def forward_pass(tokens_b, positions_b, weight_set, allowed):
    gathered, kv_mat, scales = unpack(weight_set)
    q_mat, o_mat, gate_mat, up_mat, down_mat = gathered
    scale_ai, scale_ao, scale_fi, scale_fo, scale_q, scale_k = scales
    inputs = tokens_b.astype(jnp.float32)
    cos_t, sin_t = angles(positions_b, HEAD)
    in_hat, in_fac = normalize(inputs)
    normed = (in_hat * scale_ai).astype(jnp.bfloat16)
    q_raw = product("scd,de->sce", normed, q_mat)
    kv_raw = product("scd,de->sce", normed, kv_mat)
    q_hat, q_fac = normalize(q_raw)
    queries = (rotate(q_hat * scale_q, cos_t, sin_t) * QSCALE).astype(jnp.bfloat16)
    k_hat, k_fac = normalize(kv_raw[..., :HEAD])
    keys_local = rotate(k_hat * scale_k, cos_t, sin_t).astype(jnp.bfloat16)
    values_local = kv_raw[..., HEAD:].astype(jnp.bfloat16)
    both_local = jnp.concatenate([keys_local, values_local], axis=-1)
    key_value = lax.all_gather(both_local, "seq", axis=1, tiled=True)
    key_all = key_value[..., :HEAD]
    value_all = key_value[..., HEAD:]
    scores = product("sqd,skd->sqk", queries, key_all)
    scores = jnp.where(allowed[None], scores, MASKED)
    peak_v = jnp.max(scores, axis=-1, keepdims=True)
    expo_v = jnp.exp(scores - peak_v)
    total_v = jnp.sum(expo_v, axis=-1, keepdims=True)
    probs = expo_v / total_v
    log_total = (peak_v + jnp.log(total_v))[..., 0]
    probs_low = probs.astype(jnp.bfloat16)
    attended = product("sqk,skd->sqd", probs_low, value_all).astype(jnp.bfloat16)
    partial_b = product("sce,ed->scd", attended, o_mat)
    branch = sum_tensor(partial_b)
    br_hat, br_fac = normalize(branch)
    middle = inputs + br_hat * scale_ao
    mid_hat, mid_fac = normalize(middle)
    normed_ffn = (mid_hat * scale_fi).astype(jnp.bfloat16)
    gate_v = product("scd,df->scf", normed_ffn, gate_mat)
    upper_v = product("scd,df->scf", normed_ffn, up_mat)
    acted = gelu_mix(gate_v, upper_v).astype(jnp.bfloat16)
    partial_f = product("scf,fd->scd", acted, down_mat)
    ffn_out = sum_tensor(partial_f)
    ffn_hat, ffn_fac = normalize(ffn_out)
    result_b = (middle + ffn_hat * scale_fo).astype(jnp.bfloat16)
    saved = (
        cos_t,
        sin_t,
        in_hat,
        in_fac,
        normed,
        q_hat,
        q_fac,
        k_hat,
        k_fac,
        queries,
        key_all,
        value_all,
        probs,
        probs_low,
        attended,
        br_hat,
        br_fac,
        mid_hat,
        mid_fac,
        normed_ffn,
        gate_v,
        upper_v,
        acted,
        ffn_hat,
        ffn_fac,
        log_total,
        keys_local,
        values_local,
    )
    return (result_b, saved)


def backward_pass(grad_b, saved, weight_set):
    gathered, kv_mat, scales = unpack(weight_set)
    q_mat, o_mat, gate_mat, up_mat, down_mat = gathered
    scale_ai, scale_ao, scale_fi, scale_fo, scale_q, scale_k = scales
    (
        cos_t,
        sin_t,
        in_hat,
        in_fac,
        normed,
        q_hat,
        q_fac,
        k_hat,
        k_fac,
        queries,
        key_all,
        value_all,
        probs,
        probs_low,
        attended,
        br_hat,
        br_fac,
        mid_hat,
        mid_fac,
        normed_ffn,
        gate_v,
        upper_v,
        acted,
        ffn_hat,
        ffn_fac,
        log_total,
        keys_local,
        values_local,
    ) = saved
    back = grad_b.astype(jnp.float32)
    g_fo = share_sum(back * ffn_hat)
    d_ffn = norm_back(ffn_hat, ffn_fac, back * scale_fo).astype(jnp.bfloat16)
    g_down = product("scf,scd->fd", acted, d_ffn)
    d_acted = product("scd,fd->scf", d_ffn, down_mat)
    unused_out, pull_back = jax.vjp(gelu_mix, gate_v, upper_v)
    d_gate, d_up = pull_back(d_acted)
    d_gate = d_gate.astype(jnp.bfloat16)
    d_up = d_up.astype(jnp.bfloat16)
    g_gate = product("scd,scf->df", normed_ffn, d_gate)
    g_up = product("scd,scf->df", normed_ffn, d_up)
    d_nffn = product("scf,df->scd", d_gate, gate_mat) + product("scf,df->scd", d_up, up_mat)
    g_fi = all_rows(d_nffn * mid_hat)
    d_nffn = sum_tensor(d_nffn)
    d_middle = back + norm_back(mid_hat, mid_fac, d_nffn * scale_fi)
    g_ao = share_sum(d_middle * br_hat)
    d_branch = norm_back(br_hat, br_fac, d_middle * scale_ao).astype(jnp.bfloat16)
    g_out = product("sce,scd->ed", attended, d_branch)
    d_att = product("scd,ed->sce", d_branch, o_mat).astype(jnp.bfloat16)
    d_probs = product("sqd,skd->sqk", d_att, value_all)
    row_dot = jnp.sum(probs * d_probs, axis=-1)
    d_scores = (probs * (d_probs - row_dot[..., None])).astype(jnp.bfloat16)
    d_queries = product("sqk,skd->sqd", d_scores, key_all)
    key_terms = product("sqk,sqd->skd", d_scores, queries)
    value_terms = product("sqk,sqd->skd", probs_low, d_att)
    d_keys, d_values = (
        lax.psum_scatter(
            key_terms.astype(jnp.bfloat16), "seq", scatter_dimension=1, tiled=True
        ).astype(jnp.float32),
        lax.psum_scatter(
            value_terms.astype(jnp.bfloat16), "seq", scatter_dimension=1, tiled=True
        ).astype(jnp.float32),
    )
    dq_turn = rotate_back(d_queries * QSCALE, cos_t, sin_t)
    g_q = all_rows(dq_turn * q_hat)
    d_qraw = norm_back(q_hat, q_fac, dq_turn * scale_q).astype(jnp.bfloat16)
    dk_turn = rotate_back(d_keys, cos_t, sin_t)
    g_k = all_rows(dk_turn * k_hat)
    d_kvraw = jnp.concatenate(
        [norm_back(k_hat, k_fac, dk_turn * scale_k), d_values], axis=-1
    ).astype(jnp.bfloat16)
    g_qmat = product("scd,sce->de", normed, d_qraw)
    g_kv = product("scd,sce->de", normed, d_kvraw)
    d_normed = product("sce,de->scd", d_qraw, q_mat) + product("sce,de->scd", d_kvraw, kv_mat)
    g_ai = all_rows(d_normed * in_hat)
    d_normed = sum_tensor(d_normed)
    d_input = (d_middle + norm_back(in_hat, in_fac, d_normed * scale_ai)).astype(jnp.bfloat16)
    grads = (g_qmat, g_kv, g_out, g_gate, g_up, g_down, g_ai, g_ao, g_fi, g_fo, g_q, g_k)
    return (d_input, grads)


def body(
    tokens,
    positions,
    out_grad,
    q_weight,
    kv_weight,
    o_weight,
    gate_weight,
    up_weight,
    down_weight,
    attn_in_gain,
    attn_out_gain,
    ffn_in_gain,
    ffn_out_gain,
    q_gain,
    k_gain,
):
    matrices = (q_weight, o_weight, gate_weight, up_weight, down_weight)
    small_set = (kv_weight, attn_in_gain, attn_out_gain, ffn_in_gain, ffn_out_gain, q_gain, k_gain)
    per_batch = tokens.shape[0] // MICRO
    local_len = tokens.shape[1]
    hidden_n = gate_weight.shape[1]
    seq_full = local_len * lax.axis_size("seq")
    row_ids = lax.axis_index("seq") * local_len + jnp.arange(local_len, dtype=jnp.int32)
    all_ids = jnp.arange(seq_full, dtype=jnp.int32)
    allowed = all_ids[None, :] <= row_ids[:, None]
    totals = (
        jnp.zeros((D, HEAD), jnp.float32),
        jnp.zeros((D, 2 * HEAD), jnp.float32),
        jnp.zeros((HEAD, D), jnp.float32),
        jnp.zeros((D, hidden_n), jnp.float32),
        jnp.zeros((D, hidden_n), jnp.float32),
        jnp.zeros((hidden_n, D), jnp.float32),
        jnp.zeros((D,), jnp.float32),
        jnp.zeros((D,), jnp.float32),
        jnp.zeros((D,), jnp.float32),
        jnp.zeros((D,), jnp.float32),
        jnp.zeros((HEAD,), jnp.float32),
        jnp.zeros((HEAD,), jnp.float32),
    )
    results = []
    input_grads = []
    for batch_no in range(MICRO):
        front_set = fetch_front(matrices, small_set)
        first_row = batch_no * per_batch
        last_row = first_row + per_batch
        result_b, saved = forward_pass(
            tokens[first_row:last_row], positions[first_row:last_row], front_set, allowed
        )
        back_set = fetch_back(matrices, small_set)
        d_input, grads = backward_pass(out_grad[first_row:last_row], saved, back_set)
        totals = tuple((jnp.add(running, added) for running, added in zip(totals, grads)))
        results.append(result_b)
        input_grads.append(d_input)
    main_set = (
        lax.psum_scatter(
            totals[0].astype(jnp.bfloat16), ("dp", "seq"), scatter_dimension=0, tiled=True
        ).astype(jnp.float32),
        lax.psum_scatter(
            totals[2].astype(jnp.bfloat16), ("dp", "seq"), scatter_dimension=1, tiled=True
        ).astype(jnp.float32),
        lax.psum_scatter(
            totals[3].astype(jnp.bfloat16), ("dp", "seq"), scatter_dimension=0, tiled=True
        ).astype(jnp.float32),
        lax.psum_scatter(
            totals[4].astype(jnp.bfloat16), ("dp", "seq"), scatter_dimension=0, tiled=True
        ).astype(jnp.float32),
        lax.psum_scatter(
            totals[5].astype(jnp.bfloat16), ("dp", "seq"), scatter_dimension=1, tiled=True
        ).astype(jnp.float32),
    )
    shared_set = (
        lax.psum_scatter(totals[1], ("dp", "seq", "tensor"), scatter_dimension=0, tiled=True),
        lax.psum_scatter(totals[6], ("dp", "seq", "tensor"), scatter_dimension=0, tiled=True),
        lax.psum_scatter(totals[7], ("dp", "seq", "tensor"), scatter_dimension=0, tiled=True),
        lax.psum_scatter(totals[8], ("dp", "seq", "tensor"), scatter_dimension=0, tiled=True),
        lax.psum_scatter(totals[9], ("dp", "seq", "tensor"), scatter_dimension=0, tiled=True),
        lax.psum_scatter(totals[10], ("dp", "seq", "tensor"), scatter_dimension=0, tiled=True),
        lax.psum_scatter(totals[11], ("dp", "seq", "tensor"), scatter_dimension=0, tiled=True),
    )
    return (
        jnp.concatenate(results, axis=0),
        jnp.concatenate(input_grads, axis=0),
        main_set[0],
        shared_set[0],
        main_set[1],
        main_set[2],
        main_set[3],
        main_set[4],
        shared_set[1],
        shared_set[2],
        shared_set[3],
        shared_set[4],
        shared_set[5],
        shared_set[6],
    )


def solution(mesh):
    in_specs = (
        P("dp", "seq", None),
        P("dp", "seq"),
        P("dp", "seq", None),
        P(("dp", "seq"), "tensor"),
        P(("dp", "seq", "tensor"), None),
        P("tensor", ("dp", "seq")),
        P(("dp", "seq"), "tensor"),
        P(("dp", "seq"), "tensor"),
        P("tensor", ("dp", "seq")),
        P(("dp", "seq", "tensor")),
        P(("dp", "seq", "tensor")),
        P(("dp", "seq", "tensor")),
        P(("dp", "seq", "tensor")),
        P(("dp", "seq", "tensor")),
        P(("dp", "seq", "tensor")),
    )
    out_specs = (
        P("dp", "seq", None),
        P("dp", "seq", None),
        P(("dp", "seq"), "tensor"),
        P(("dp", "seq", "tensor"), None),
        P("tensor", ("dp", "seq")),
        P(("dp", "seq"), "tensor"),
        P(("dp", "seq"), "tensor"),
        P("tensor", ("dp", "seq")),
        P(("dp", "seq", "tensor")),
        P(("dp", "seq", "tensor")),
        P(("dp", "seq", "tensor")),
        P(("dp", "seq", "tensor")),
        P(("dp", "seq", "tensor")),
        P(("dp", "seq", "tensor")),
    )
    return jax.shard_map(body, mesh=mesh, in_specs=in_specs, out_specs=out_specs, check_vma=False)
```

profile of v0, /device:TPU:0, one launch (start us, length us, event | category | flops | bytes accessed | tf_op | source)
XLA Modules:
  0.0 1222.0 jit_solution(10548067871685303308)
XLA Ops:
  12.6 42.4 %all-reduce.19 = (bf16[1152]{0:T(1024)(128)(2,1)S(1)}, bf16[256]{0:T(256)(128)(2,1)S(1)}, bf16[256]{0:T(256)(128)(2,1)S(1)}, bf16[1152]{0:T(1024)(128)(2,1)}, bf...) all-reduce(bf16[1152]{0:T(1024)(128)(2,1)S(1)} %dynamic-update-slic, ...), channel_id=1, replica_groups=mesh['dp'=4,'seq'=2,'tensor'=4] {'dp','seq','tensor'}, use_global_device_ids=true, to_apply=%add | all-reduce | flops 5120 | bytes 20480
  56.2 31.7 %all_gather.29 = bf16[1152,256]{1,0:T(8,128)(2,1)S(1)} all-gather(bf16[144,256]{1,0:T(8,128)(2,1)S(1)} %copy-done.85), channel_id=1, replica_groups=mesh['dp'=4,'seq'=2,'tensor'=4] {'dp','seq'}, dimensions={0}, use_global_device_ids=true | all-gather | bytes 663552 | tf_op jit(solution)/shard_map/all_gather | solution.py:74
  109.3 32.1 %all_gather.34 = bf16[256,1152]{0,1:T(8,128)(2,1)S(1)} all-gather(bf16[256,144]{0,1:T(8,128)(2,1)} %param.20), channel_id=1, replica_groups=mesh['dp'=4,'seq'=2,'tensor'=4] {'dp','seq'}, dimensions={1}, use_global_device_ids=true | all-gather | bytes 663552 | tf_op jit(solution)/shard_map/all_gather | solution.py:75
  141.4 6.9 fusion.82
  148.4 2.9 fusion.50
  153.7 3.0 fusion.53
  168.4 91.1 %all-reduce.31.cloned.1.call-done = (f32[1,512,1152]{2,1,0:T(8,128)}, f32[1,512,1152]{2,1,0:T(8,128)}) async-done(((f32[1,512,1152]{2,1,0:T(8,128)}, f32[1,512,1152]{2,1,0:T(8,128)}), (f32[1,512,1152]{2,1,0:T(8,128)}, f32[1,512,1152]{2,1,0:T(8,128)})) %all-reduce.31.cloned.1.call-update) | async-done | bytes 4718608 | tf_op jit(solution)/shard_map/psum | solution.py:69
  262.6 4.9 multiply_reduce_fusion.12
  270.8 7.0 fusion.147
  277.8 4.3 fusion.146
  282.1 30.5 %all-gather.12.cloned.1.call-done = bf16[1152,1728]{1,0:T(8,128)(2,1)} async-done(((bf16[144,1728]{1,0:T(8,128)(2,1)}), bf16[1152,1728]{1,0:T(8,128)(2,1)}) %all-gather.12.cloned.1.call-update) | async-done | bytes 3981328 | tf_op jit(solution)/shard_map/all_gather | solution.py:77
  312.5 9.4 multiply_convert_fusion.2
  322.0 6.2 multiply_convert_fusion.3
  328.2 57.0 %all-gather.14.cloned.1.call-done = bf16[1728,1152]{0,1:T(8,128)(2,1)} async-done(((bf16[1728,144]{0,1:T(8,128)(2,1)}), bf16[1728,1152]{0,1:T(8,128)(2,1)}) %all-gather.14.cloned.1.call-update) | async-done | bytes 3981328 | tf_op jit(solution)/shard_map/all_gather | solution.py:78
  385.2 6.8 convolution_bitcast_fusion
  392.0 4.0 convolution_bitcast_fusion.2
  396.1 92.8 %all-reduce.29.cloned.1.call-done = (f32[1,512,1152]{2,1,0:T(8,128)}, f32[1,512,1152]{2,1,0:T(8,128)}) async-done(((f32[1,512,1152]{2,1,0:T(8,128)}, f32[1,512,1152]{2,1,0:T(8,128)}), (f32[1,512,1152]{2,1,0:T(8,128)}, f32[1,512,1152]{2,1,0:T(8,128)})) %all-reduce.29.cloned.1.call-update) | async-done | bytes 4718608 | tf_op jit(solution)/shard_map/psum | solution.py:69
  502.3 5.7 multiply_convert_fusion
  511.5 4.1 fusion.27
  515.6 7.4 multiply_convert_fusion.1
  525.6 4.1 fusion.26
  529.8 94.5 %all-reduce.27.cloned.1.call-done = (f32[1,512,1152]{2,1,0:T(8,128)}, f32[1,512,1152]{2,1,0:T(8,128)}) async-done(((f32[1,512,1152]{2,1,0:T(8,128)}, f32[1,512,1152]{2,1,0:T(8,128)}), (f32[1,512,1152]{2,1,0:T(8,128)}, f32[1,512,1152]{2,1,0:T(8,128)})) %all-reduce.27.cloned.1.call-update) | async-done | bytes 4718608 | tf_op jit(solution)/shard_map/psum | solution.py:69
  624.3 6.3 multiply_reduce_fusion
  650.2 2.9 fusion.57
  656.9 3.4 multiply_reduce_fusion.19
  667.8 4.2 multiply_reduce_fusion.18
  687.1 2.9 convert_multiply_fusion.6
  690.1 3.9 multiply_reduce_fusion.17
  694.0 6.1 multiply_reduce_fusion.16
  703.0 4.2 fusion.29
  709.8 4.2 fusion.28
  714.3 4.3 fusion.153
  718.7 4.4 fusion.1
  723.2 4.3 fusion.154
  727.5 4.4 fusion.2
  732.3 4.3 fusion.155
  736.7 4.4 fusion.3
  741.2 4.1 slice_convert_fusion
  748.8 83.7 %fusion = f32[40,512]{1,0:T(8,128)} fusion(f32[1152,512]{1,0:T(8,128)} %convolution_add_fusion.3), kind=kCustom, calls=%all-reduce-scatter | all-reduce-scatter fusion | flops 655361 | bytes 2441216
  837.1 2.9 pad_maximum_fusion
  848.1 2.9 concatenate.182
  854.8 83.0 %all-reduce.25.cloned.1.call-done = (f32[1,512,1152]{2,1,0:T(8,128)}, f32[1,512,1152]{2,1,0:T(8,128)}) async-done(((f32[1,512,1152]{2,1,0:T(8,128)}, f32[1,512,1152]{2,1,0:T(8,128)}), (f32[1,512,1152]{2,1,0:T(8,128)}, f32[1,512,1152]{2,1,0:T(8,128)})) %all-reduce.25.cloned.1.call-update) | async-done | bytes 4718608 | tf_op jit(solution)/shard_map/psum | solution.py:69
  937.8 4.4 fusion.33
  942.3 42.4 %all-reduce.14 = (f32[1152]{0:T(1024)S(1)}, f32[1152]{0:T(1024)S(1)}, f32[1152]{0:T(1024)S(1)}, f32[1152]{0:T(1024)S(1)}, f32[256]{0:T(256)S(1)}, /*index=5*/f32[256]{0:T(256)S(1)}) all-reduce(f32[1152]{0:T(1024)S(1)} %add.384, f32[1152]{0:T(1024)S(1)} %add.386, ...), channel_id=12, replica_groups=mesh['dp'=4,'seq'=2,'tensor'=4] {'dp','seq','tensor'}, use_global_device_ids=true, to_apply=%region_50.51.clone | all-reduce | flops 5120 | bytes 40960
  988.2 4.4 fusion.37
  994.3 35.9 %reduce-scatter.24.cloned.1.call-done = bf16[144,1728]{1,0:T(8,128)(2,1)} async-done(((bf16[1152,1728]{1,0:T(8,128)(2,1)}), bf16[144,1728]{1,0:T(8,128)(2,1)}) %reduce-scatter.24.cloned.1.call-update) | async-done | bytes 497680 | tf_op jit(solution)/shard_map/reduce_scatter | solution.py:338
  1032.2 89.2 %reduce-scatter.26.cloned.1.call-done = bf16[144,1728]{1,0:T(8,128)(2,1)} async-done(((bf16[1152,1728]{1,0:T(8,128)(2,1)}), bf16[144,1728]{1,0:T(8,128)(2,1)}) %reduce-scatter.26.cloned.1.call-update) | async-done | bytes 497680 | tf_op jit(solution)/shard_map/reduce_scatter | solution.py:341
  1123.5 88.7 %reduce-scatter.28.cloned.1.call-done = bf16[1728,144]{0,1:T(8,128)(2,1)} async-done(((bf16[1728,1152]{0,1:T(8,128)(2,1)}), bf16[1728,144]{0,1:T(8,128)(2,1)}) %reduce-scatter.28.cloned.1.call-update) | async-done | bytes 497680 | tf_op jit(solution)/shard_map/reduce_scatter | solution.py:344
  (495 shorter events, 149.0 us)
Async XLA Ops:
  8.0 79.9 %copy-start.5 = (bf16[2,512,1152]{2,1,0:T(8,128)(2,1)S(1)}, bf16[2,512,1152]{2,1,0:T(8,128)(2,1)}, u32[]{:S(2)}) copy-start(bf16[2,512,1152]{2,1,0:T(8,128)(2,1)} %param.15) | copy-start | bytes 7077892
  8.1 48.1 %copy-start.85 = (bf16[144,256]{1,0:T(8,128)(2,1)S(1)}, bf16[144,256]{1,0:T(8,128)(2,1)}, u32[]{:S(2)}) copy-start(bf16[144,256]{1,0:T(8,128)(2,1)} %param.18) | copy-start | bytes 221188
  8.1 84.0 %all-gather.18.cloned.1.call-start = ((), (), s32[]{:S(2)}) async-start(), calls=%async_computation.23 | async-start | bytes 1351680 | tf_op jit(solution)/shard_map/all_gather | solution.py:81
  8.8 139.6 %all-gather.8.cloned.1.call-start = ((), (), s32[]{:S(2)}) async-start(), calls=%async_computation.9 | async-start | bytes 1572864 | tf_op jit(solution)/shard_map/all_gather | solution.py:134
  56.1 34.8 %copy-start.95 = (f32[512]{0:T(512)}, f32[512]{0:T(512)S(1)}, u32[]{:S(2)}) copy-start(f32[512]{0:T(512)S(1)} %get-tuple-element.142) | copy-start | bytes 6148
  56.1 34.7 %copy-start.115 = (f32[512]{0:T(512)}, f32[512]{0:T(512)S(1)}, u32[]{:S(2)}) copy-start(f32[512]{0:T(512)S(1)} %get-tuple-element.143) | copy-start | bytes 6148
  89.4 52.0 %copy-start.89 = (f32[512]{0:T(512)}, f32[512]{0:T(512)S(1)}, u32[]{:S(2)}) copy-start(f32[512]{0:T(512)S(1)} %add_rsqrt_fusion.10) | copy-start | bytes 6148
  90.9 50.5 %copy-start.87 = (f32[512]{0:T(512)}, f32[512]{0:T(512)S(1)}, u32[]{:S(2)}) copy-start(f32[512]{0:T(512)S(1)} %add_rsqrt_fusion.4) | copy-start | bytes 6148
  101.0 52.7 %all-gather.16.cloned.1.call-start = ((), (), s32[]{:S(2)}) async-start(), calls=%async_computation.13 | async-start | bytes 1572864 | tf_op jit(solution)/shard_map/all_gather | solution.py:134
  105.2 36.1 %copy-start.44 = (f32[512,128]{0,1:T(8,128)S(1)}, f32[512,128]{0,1:T(8,128)}, u32[]{:S(2)}) copy-start(f32[512,128]{0,1:T(8,128)} %get-tuple-element.123) | copy-start | bytes 786436
  105.3 36.1 %copy-start.46 = (f32[512,128]{0,1:T(8,128)S(1)}, f32[512,128]{0,1:T(8,128)}, u32[]{:S(2)}) copy-start(f32[512,128]{0,1:T(8,128)} %get-tuple-element.110) | copy-start | bytes 786436
  107.3 34.2 %copy-start.105 = (f32[256]{0:T(256)S(1)}, f32[256]{0:T(256)}, u32[]{:S(2)}) copy-start(f32[256]{0:T(256)} %convert_add_fusion.7) | copy-start | bytes 3076
  108.1 151.3 %all-reduce.31.cloned.1.call-start = ((), (), s32[]{:S(2)}) async-start(), calls=%async_computation.27 | async-start | bytes 9437184 | tf_op jit(solution)/shard_map/psum | solution.py:69
  141.4 21.7 %copy-start.37 = (bf16[256,1152]{0,1:T(8,128)(2,1)}, bf16[256,1152]{0,1:T(8,128)(2,1)S(1)}, u32[]{:S(2)}) copy-start(bf16[256,1152]{0,1:T(8,128)(2,1)S(1)} %all_gather.34) | copy-start | bytes 1769476
  165.1 105.7 %all-gather.10.cloned.1.call-start = ((), (), s32[]{:S(2)}) async-start(), calls=%async_computation.10 | async-start | bytes 4644864 | tf_op jit(solution)/shard_map/all_gather | solution.py:76
  165.7 146.9 %all-gather.12.cloned.1.call-start = ((), (), s32[]{:S(2)}) async-start(), calls=%async_computation.11 | async-start | bytes 4644864 | tf_op jit(solution)/shard_map/all_gather | solution.py:77
  166.3 218.9 %all-gather.14.cloned.1.call-start = ((), (), s32[]{:S(2)}) async-start(), calls=%async_computation.12 | async-start | bytes 4644864 | tf_op jit(solution)/shard_map/all_gather | solution.py:78
  166.8 322.0 %all-reduce.29.cloned.1.call-start = ((), (), s32[]{:S(2)}) async-start(), calls=%async_computation.26 | async-start | bytes 9437184 | tf_op jit(solution)/shard_map/psum | solution.py:69
  312.5 9.5 copy-start.63
  312.5 9.5 copy-start.131
  312.5 9.5 copy-start.149
  396.0 228.2 %all-reduce.27.cloned.1.call-start = ((), (), s32[]{:S(2)}) async-start(), calls=%async_computation.25 | async-start | bytes 9437184 | tf_op jit(solution)/shard_map/psum | solution.py:69
  494.7 7.5 copy-start.152
  498.2 9.8 copy-start.58
  498.2 17.4 %copy-start.60 = (bf16[512,1152]{1,0:T(8,128)(2,1)}, bf16[512,1152]{1,0:T(8,128)(2,1)S(1)}, u32[]{:S(2)}) copy-start(bf16[512,1152]{1,0:T(8,128)(2,1)S(1)} %get-tuple-element.77) | copy-start | bytes 3538948
  529.7 153.6 %reduce-scatter.16.cloned.1.call-start = ((), (), s32[]{:S(2)}) async-start(), calls=%async_computation.16 | async-start | bytes 786432 | tf_op jit(solution)/shard_map/reduce_scatter | solution.py:252
  624.3 7.2 copy-start.13
  624.3 7.9 copy-start.20
  624.3 8.5 copy-start.21
  624.3 8.5 copy-start.82
  624.3 8.5 copy-start.102
  624.3 8.5 copy-start.104
  644.4 42.6 %reduce-scatter.12.cloned.1.call-start = ((), (), s32[]{:S(2)}) async-start(), calls=%async_computation.14 | async-start | bytes 786432 | tf_op jit(solution)/shard_map/reduce_scatter | solution.py:252
  649.8 53.2 %reduce-scatter.18.cloned.1.call-start = ((), (), s32[]{:S(2)}) async-start(), calls=%async_computation.17 | async-start | bytes 786432 | tf_op jit(solution)/shard_map/reduce_scatter | solution.py:255
  660.4 49.5 %reduce-scatter.14.cloned.1.call-start = ((), (), s32[]{:S(2)}) async-start(), calls=%async_computation.15 | async-start | bytes 786432 | tf_op jit(solution)/shard_map/reduce_scatter | solution.py:255
  667.8 183.9 %reduce-scatter.20.cloned.1.call-start = ((), (), s32[]{:S(2)}) async-start(), calls=%async_computation.18 | async-start | bytes 663552 | tf_op jit(solution)/shard_map/reduce_scatter | solution.py:332
  675.5 177.7 %reduce-scatter.22.cloned.1.call-start = ((), (), s32[]{:S(2)}) async-start(), calls=%async_computation.19 | async-start | bytes 663552 | tf_op jit(solution)/shard_map/reduce_scatter | solution.py:335
  683.1 254.7 %all-reduce.25.cloned.1.call-start = ((), (), s32[]{:S(2)}) async-start(), calls=%async_computation.24 | async-start | bytes 9437184 | tf_op jit(solution)/shard_map/psum | solution.py:69
  686.2 7.8 copy-start.99
  690.1 10.1 copy-start.119
  714.0 316.1 %reduce-scatter.24.cloned.1.call-start = ((), (), s32[]{:S(2)}) async-start(), calls=%async_computation.20 | async-start | bytes 4644864 | tf_op jit(solution)/shard_map/reduce_scatter | solution.py:338
  723.1 398.3 %reduce-scatter.26.cloned.1.call-start = ((), (), s32[]{:S(2)}) async-start(), calls=%async_computation.21 | async-start | bytes 4644864 | tf_op jit(solution)/shard_map/reduce_scatter | solution.py:341
  732.0 480.2 %reduce-scatter.28.cloned.1.call-start = ((), (), s32[]{:S(2)}) async-start(), calls=%async_computation.22 | async-start | bytes 4644864 | tf_op jit(solution)/shard_map/reduce_scatter | solution.py:344
  748.8 88.2 %copy-start.41 = (bf16[1,512,1152]{2,1,0:T(8,128)(2,1)S(1)}, bf16[1,512,1152]{2,1,0:T(8,128)(2,1)}, u32[]{:S(2)}) copy-start(bf16[1,512,1152]{2,1,0:T(8,128)(2,1)} %get-tuple-element.78) | copy-start | bytes 3538948
  832.6 14.3 %collective-permute-start.2 = (f32[40,512]{1,0:T(8,128)}, f32[40,512]{1,0:T(8,128)S(1)}, u32[]{:S(2)}, u32[]{:S(2)}) collective-permute-start(f32[40,512]{1,0:T(8,128)} %fusion), channel_id=1, source_target_pairs={{0,3},{1,4},{2,5},{3,6},{4,7},{5,8},{6,9},{7,10},{8,11},{9,12},{10... | collective-permute-start | bytes 245768
  833.8 13.0 %collective-permute-start.1 = (f32[40,512]{1,0:T(8,128)}, f32[40,512]{1,0:T(8,128)S(1)}, u32[]{:S(2)}, u32[]{:S(2)}) collective-permute-start(f32[40,512]{1,0:T(8,128)} %fusion), channel_id=1, source_target_pairs={{0,2},{1,3},{2,4},{3,5},{4,6},{5,7},{6,8},{7,9},{8,10},{9,11},{10,... | collective-permute-start | bytes 245768
  835.1 13.0 %collective-permute-start = (f32[40,512]{1,0:T(8,128)}, f32[40,512]{1,0:T(8,128)}, u32[]{:S(2)}, u32[]{:S(2)}) collective-permute-start(f32[40,512]{1,0:T(8,128)} %fusion), channel_id=1, source_target_pairs={{0,1},{1,2},{2,3},{3,4},{4,5},{5,6},{6,7},{7,8},{8,9},{9,10},{10,1... | collective-permute-start | bytes 245768
  844.1 2.7 collective-permute-start.3
  (128 other events, 449.2 us)
Sparse Core Ops, SparseCore 0:
  11.8 57.4 all-gather.17
  101.1 28.5 all-gather.7
  131.9 21.7 all-gather.15
  165.2 94.1 all-reduce.30
  396.2 92.6 all-reduce.28
  529.9 94.3 all-reduce.26
  644.5 14.7 reduce-scatter.15
  661.6 14.5 reduce-scatter.11
  678.4 14.5 reduce-scatter.17
  695.2 14.5 reduce-scatter.13
  713.7 62.1 reduce-scatter.19
  779.9 62.2 reduce-scatter.21
  844.6 93.1 all-reduce.24
  941.2 88.8 reduce-scatter.23
  1034.0 87.3 reduce-scatter.25
  1124.8 87.3 reduce-scatter.27
Sparse Core Ops, SparseCore 1:
  167.8 72.1 all-gather.9
  241.9 70.5 all-gather.11
  314.6 70.5 all-gather.13
where the time goes:
time: 1230 us; the launch traced here: 1220 us
  waiting for transfers between devices  670 us (54%)
  blocking collectives  232 us (19%)
  matrix products  143 us (12%)
  other arithmetic  119 us (10%)
  local copies, waits for them, and re-layouts  31.8 us (3%)
  between operations  18 us (1%)
    psum x4, waiting for transfers between devices, sum_tensor(): return lax.psum(values, 'tensor')  361 us
    unnamed x3, blocking collectives  169 us
    dot_general x48, matrix products, product(): jnp.einsum(pattern, left_m, right_m, preferred_element_type=jnp.float32)  143 us
    reduce_scatter x1, waiting for transfers between devices, body(): lax.psum_scatter(totals[4].astype(jnp.bfloat16), ('dp', 'seq'), scatter_d...  89.2 us
    reduce_scatter x1, waiting for transfers between devices, body(): lax.psum_scatter(totals[5].astype(jnp.bfloat16), ('dp', 'seq'), scatter_d...  88.7 us
    all_gather x1, waiting for transfers between devices, fetch_front(): lax.all_gather(matrices[4], ('dp', 'seq'), axis=1, tiled=True)  57 us
    reduce_scatter x1, waiting for transfers between devices, body(): lax.psum_scatter(totals[3].astype(jnp.bfloat16), ('dp', 'seq'), scatter_d...  35.9 us
    all_gather x1, blocking collectives, fetch_front(): lax.all_gather(matrices[1], ('dp', 'seq'), axis=1, tiled=True)  32.1 us
  transfers between devices with their start and end apart: 23, of which 11 were waited for; matrix products, arithmetic and copies ran while one was open for 23% of the time, Pallas kernels for 0%

commit v1 on v0

v1 whole, which is shorter than its diff:
```python
import jax
import jax.numpy as jnp
from jax import lax
from jax.sharding import PartitionSpec as P

EPS = 1e-06
QSCALE = 0.0625
MASKED = -1e30
LOW = jnp.bfloat16
F32 = jnp.float32
ALL = ("dp", "seq", "tensor")


def normalize(values):
    factor = lax.rsqrt(jnp.mean(values * values, axis=-1, keepdims=True) + EPS)
    return (values * factor, factor)


def norm_back(scaled, factor, upstream):
    return factor * (upstream - scaled * jnp.mean(upstream * scaled, axis=-1, keepdims=True))


def angles(positions, width_n):
    half_w = width_n // 2
    freq_t = 1000000.0 ** (-(jnp.arange(half_w, dtype=F32) * 2.0 / width_n))
    turn_t = positions.astype(F32)[..., None] * freq_t
    return (jnp.cos(turn_t), jnp.sin(turn_t))


def rotate(values, cos_t, sin_t):
    half_w = values.shape[-1] // 2
    low_v, high_v = values[..., :half_w], values[..., half_w:]
    return jnp.concatenate(
        [low_v * cos_t - high_v * sin_t, high_v * cos_t + low_v * sin_t], axis=-1
    )


def rotate_back(values, cos_t, sin_t):
    half_w = values.shape[-1] // 2
    low_v, high_v = values[..., :half_w], values[..., half_w:]
    return jnp.concatenate(
        [low_v * cos_t + high_v * sin_t, high_v * cos_t - low_v * sin_t], axis=-1
    )


def product(pattern, left_m, right_m):
    return jnp.einsum(pattern, left_m, right_m, preferred_element_type=F32)


def gelu_mix(gate_v, upper_v):
    return jax.nn.gelu(gate_v, approximate=True) * upper_v


def swap(values):
    return lax.ppermute(values, "seq", [(0, 1), (1, 0)])


def in_order(mine, theirs, axis):
    first = lax.axis_index("seq") == 0
    return jnp.stack(
        [jnp.where(first, mine, theirs), jnp.where(first, theirs, mine)], axis=axis
    )


def gather_rows(shard):
    seq_n = lax.axis_size("seq")
    if seq_n != 2:
        return lax.all_gather(shard, ("dp", "seq"), axis=0, tiled=True)
    mine = lax.all_gather(shard, "dp", axis=0, tiled=False)
    both = in_order(mine, swap(mine), 1)
    return both.reshape(-1, shard.shape[-1])


def scatter_rows(total):
    seq_n = lax.axis_size("seq")
    total = total.astype(LOW)
    if seq_n != 2:
        return lax.psum_scatter(
            total, ("dp", "seq"), scatter_dimension=0, tiled=True
        ).astype(F32)
    dp_n = lax.axis_size("dp")
    me = lax.axis_index("seq")
    parts = total.reshape(dp_n, 2, -1, total.shape[-1])
    away = lax.dynamic_index_in_dim(parts, 1 - me, 1, keepdims=False)
    stay = lax.dynamic_index_in_dim(parts, me, 1, keepdims=False)
    pair = (stay.astype(F32) + swap(away).astype(F32)).astype(LOW)
    pair = pair.reshape(-1, total.shape[-1])
    return lax.psum_scatter(pair, "dp", scatter_dimension=0, tiled=True).astype(F32)


def sum_share(partial):
    return lax.psum_scatter(
        partial.astype(LOW), "tensor", scatter_dimension=0, tiled=True
    ).astype(F32)


def spread(share):
    return lax.all_gather(share, "tensor", axis=0, tiled=True)


def row_sum(values):
    return jnp.sum(values.reshape(-1, values.shape[-1]), axis=0)


def body(
    tokens,
    positions,
    out_grad,
    q_weight,
    kv_weight,
    o_weight,
    gate_weight,
    up_weight,
    down_weight,
    attn_in_gain,
    attn_out_gain,
    ffn_in_gain,
    ffn_out_gain,
    q_gain,
    k_gain,
):
    batch, local_len, width = tokens.shape
    rows_n = batch * local_len
    head = q_weight.shape[1]
    seq_n, tensor_n = lax.axis_size("seq"), lax.axis_size("tensor")
    blocks_n = lax.axis_size("dp") * seq_n
    all_n = blocks_n * tensor_n
    part = width // all_n
    head_part = head // all_n
    share_n = rows_n // tensor_n
    tensor_me = lax.axis_index("tensor")

    gain_row = jnp.concatenate(
        [attn_in_gain, attn_out_gain, ffn_in_gain, ffn_out_gain, q_gain, k_gain]
    )
    gain_n = gain_row.shape[0]
    gain_row = jnp.pad(gain_row, (0, 2 * head - gain_n))[None]
    small = lax.all_gather(
        jnp.concatenate([kv_weight, gain_row], axis=0), ALL, axis=0, tiled=False
    )
    kv_mat = small[:, :part].reshape(width, 2 * head)
    gains = small[:, part, :gain_n].astype(F32)

    def gain_of(index):
        return 1.0 + gains[:, index * part : (index + 1) * part].reshape(width)

    scale_ai, scale_ao, scale_fi, scale_fo = (gain_of(index) for index in range(4))
    tail = 4 * part
    scale_q = 1.0 + gains[:, tail : tail + head_part].reshape(head)
    scale_k = 1.0 + gains[:, tail + head_part :].reshape(head)

    qo_mat = gather_rows(jnp.concatenate([q_weight, o_weight.T], axis=1))
    q_mat, o_mat = qo_mat[:, :head], qo_mat[:, head:]
    gate_mat = gather_rows(gate_weight)
    up_mat = gather_rows(up_weight)
    down_mat = gather_rows(down_weight.T)

    def share(values):
        return lax.dynamic_slice_in_dim(
            values.reshape(rows_n, width), tensor_me * share_n, share_n, 0
        ).astype(F32)

    cos_t, sin_t = angles(positions, head)
    in_hat_all, unused_fac = normalize(tokens.astype(F32))
    normed = (in_hat_all * scale_ai).astype(LOW)
    kv_raw = product("scd,de->sce", normed, kv_mat)
    k_hat, k_fac = normalize(kv_raw[..., :head])
    keys_local = rotate(k_hat * scale_k, cos_t, sin_t).astype(LOW)
    both_local = jnp.concatenate([keys_local, kv_raw[..., head:].astype(LOW)], axis=-1)
    if seq_n == 2:
        key_value = in_order(both_local, swap(both_local), 1)
        key_value = key_value.reshape(batch, 2 * local_len, 2 * head)
    else:
        key_value = lax.all_gather(both_local, "seq", axis=1, tiled=True)
    key_all, value_all = key_value[..., :head], key_value[..., head:]
    q_raw = product("scd,de->sce", normed, q_mat)
    q_hat, q_fac = normalize(q_raw)
    queries = (rotate(q_hat * scale_q, cos_t, sin_t) * QSCALE).astype(LOW)
    row_ids = lax.axis_index("seq") * local_len + jnp.arange(local_len, dtype=jnp.int32)
    all_ids = jnp.arange(seq_n * local_len, dtype=jnp.int32)
    allowed = all_ids[None, :] <= row_ids[:, None]
    scores = jnp.where(allowed[None], product("sqd,skd->sqk", queries, key_all), MASKED)
    peak_v = jnp.max(scores, axis=-1, keepdims=True)
    expo_v = jnp.exp(scores - peak_v)
    probs = expo_v / jnp.sum(expo_v, axis=-1, keepdims=True)
    probs_low = probs.astype(LOW)
    attended = product("sqk,skd->sqd", probs_low, value_all).astype(LOW)
    attended_r = attended.reshape(rows_n, head)
    branch = sum_share(product("re,de->rd", attended_r, o_mat))

    inputs = share(tokens)
    in_hat, in_fac = normalize(inputs)
    back = share(out_grad)
    br_hat, br_fac = normalize(branch)
    middle = inputs + br_hat * scale_ao
    mid_hat, mid_fac = normalize(middle)
    normed_ffn = spread((mid_hat * scale_fi).astype(LOW))
    gate_v = product("rd,df->rf", normed_ffn, gate_mat)
    upper_v = product("rd,df->rf", normed_ffn, up_mat)
    acted = gelu_mix(gate_v, upper_v).astype(LOW)
    ffn_out = sum_share(product("rf,df->rd", acted, down_mat))
    ffn_hat, ffn_fac = normalize(ffn_out)
    g_fo = row_sum(back * ffn_hat)
    d_ffn = spread(norm_back(ffn_hat, ffn_fac, back * scale_fo).astype(LOW))
    result = spread((middle + ffn_hat * scale_fo).astype(LOW)).reshape(tokens.shape)

    g_down = scatter_rows(product("rd,rf->df", d_ffn, acted)).T
    d_acted = product("rd,df->rf", d_ffn, down_mat)
    unused_out, pull_back = jax.vjp(gelu_mix, gate_v, upper_v)
    d_gate, d_up = pull_back(d_acted)
    d_gate = d_gate.astype(LOW)
    d_up = d_up.astype(LOW)
    d_nffn = sum_share(
        product("rf,df->rd", d_gate, gate_mat) + product("rf,df->rd", d_up, up_mat)
    )
    g_gate = scatter_rows(product("rd,rf->df", normed_ffn, d_gate))
    g_up = scatter_rows(product("rd,rf->df", normed_ffn, d_up))
    g_fi = row_sum(d_nffn * mid_hat)
    d_middle = back + norm_back(mid_hat, mid_fac, d_nffn * scale_fi)
    g_ao = row_sum(d_middle * br_hat)
    d_branch = spread(norm_back(br_hat, br_fac, d_middle * scale_ao).astype(LOW))

    g_out = product("rd,re->de", d_branch, attended_r)
    d_att = product("rd,de->re", d_branch, o_mat).astype(LOW).reshape(attended.shape)
    d_probs = product("sqd,skd->sqk", d_att, value_all)
    row_dot = jnp.sum(probs * d_probs, axis=-1, keepdims=True)
    d_scores = (probs * (d_probs - row_dot)).astype(LOW)
    key_terms = product("sqk,sqd->skd", d_scores, queries)
    value_terms = product("sqk,sqd->skd", probs_low, d_att)
    kv_terms = jnp.concatenate([key_terms, value_terms], axis=-1).astype(LOW)
    if seq_n == 2:
        me = lax.axis_index("seq")
        halves = kv_terms.reshape(batch, 2, local_len, 2 * head)
        away = lax.dynamic_index_in_dim(halves, 1 - me, 1, keepdims=False)
        stay = lax.dynamic_index_in_dim(halves, me, 1, keepdims=False)
        d_kv = stay.astype(F32) + swap(away).astype(F32)
    else:
        d_kv = lax.psum_scatter(kv_terms, "seq", scatter_dimension=1, tiled=True).astype(F32)
    d_queries = product("sqk,skd->sqd", d_scores, key_all)
    dq_turn = rotate_back(d_queries * QSCALE, cos_t, sin_t)
    g_q = row_sum(dq_turn * q_hat)
    d_qraw = norm_back(q_hat, q_fac, dq_turn * scale_q).astype(LOW)
    dk_turn = rotate_back(d_kv[..., :head], cos_t, sin_t)
    g_k = row_sum(dk_turn * k_hat)
    d_kvraw = jnp.concatenate(
        [norm_back(k_hat, k_fac, dk_turn * scale_k), d_kv[..., head:]], axis=-1
    ).astype(LOW)
    d_normed = product("sce,de->scd", d_qraw, q_mat) + product("sce,de->scd", d_kvraw, kv_mat)
    d_normed = sum_share(d_normed.reshape(rows_n, width))
    g_kv = product("scd,sce->de", normed, d_kvraw).astype(LOW)
    g_kv = g_kv.reshape(blocks_n, tensor_n, part, 2 * head)
    g_kv = lax.psum_scatter(g_kv, "tensor", scatter_dimension=1, tiled=False)
    g_qmat = product("scd,sce->de", normed, d_qraw)
    g_qo = jnp.concatenate([g_qmat, g_out], axis=1).astype(LOW)
    g_qo = g_qo.reshape(blocks_n, width // blocks_n, 2 * head)
    fill = jnp.zeros((blocks_n, -(width // blocks_n + part) % 16, 2 * head), LOW)
    last = jnp.concatenate([g_qo, g_kv, fill], axis=1).reshape(-1, 2 * head)
    last = scatter_rows(last)
    own_n = width // blocks_n
    g_ai = row_sum(d_normed * in_hat)
    d_input = d_middle + norm_back(in_hat, in_fac, d_normed * scale_ai)
    d_input = spread(d_input.astype(LOW)).reshape(tokens.shape)
    gain_terms = jnp.concatenate(
        [entry.reshape(all_n, -1) for entry in (g_ai, g_ao, g_fi, g_fo, g_q, g_k)], axis=1
    )
    gain_sums = lax.psum_scatter(gain_terms, ALL, scatter_dimension=0, tiled=True)[0]
    return (
        result,
        d_input,
        last[:own_n, :head],
        last[own_n : own_n + part],
        last[:own_n, head:].T,
        g_gate,
        g_up,
        g_down,
        gain_sums[:part],
        gain_sums[part : 2 * part],
        gain_sums[2 * part : 3 * part],
        gain_sums[3 * part : 4 * part],
        gain_sums[tail : tail + head_part],
        gain_sums[tail + head_part :],
    )


def solution(mesh):
    in_specs = (
        P("dp", "seq", None),
        P("dp", "seq"),
        P("dp", "seq", None),
        P(("dp", "seq"), "tensor"),
        P(("dp", "seq", "tensor"), None),
        P("tensor", ("dp", "seq")),
        P(("dp", "seq"), "tensor"),
        P(("dp", "seq"), "tensor"),
        P("tensor", ("dp", "seq")),
        P(("dp", "seq", "tensor")),
        P(("dp", "seq", "tensor")),
        P(("dp", "seq", "tensor")),
        P(("dp", "seq", "tensor")),
        P(("dp", "seq", "tensor")),
        P(("dp", "seq", "tensor")),
    )
    out_specs = (
        P("dp", "seq", None),
        P("dp", "seq", None),
        P(("dp", "seq"), "tensor"),
        P(("dp", "seq", "tensor"), None),
        P("tensor", ("dp", "seq")),
        P(("dp", "seq"), "tensor"),
        P(("dp", "seq"), "tensor"),
        P("tensor", ("dp", "seq")),
        P(("dp", "seq", "tensor")),
        P(("dp", "seq", "tensor")),
        P(("dp", "seq", "tensor")),
        P(("dp", "seq", "tensor")),
        P(("dp", "seq", "tensor")),
        P(("dp", "seq", "tensor")),
    )
    return jax.shard_map(body, mesh=mesh, in_specs=in_specs, out_specs=out_specs, check_vma=False)
```

time: 1230 us -> 895 us (0.73)
  blocking collectives: 232 us -> 59.4 us
  waiting for transfers between devices: 670 us -> 516 us
  local copies, waits for them, and re-layouts: 31.8 us -> 78.6 us
  other arithmetic: 119 us -> 76.1 us
  matrix products: 143 us -> 128 us
    psum x4 -> x0, waiting for transfers between devices: 361 us -> none  [sum_tensor(): return lax.psum(values, 'tensor')]
    ppermute x0 -> x10, waiting for transfers between devices: none -> 236 us  [swap(): return lax.ppermute(values, 'seq', [(0, 1), (1, 0)])]
    unnamed x3 -> x1, blocking collectives: 169 us -> 40.7 us
    reduce_scatter x9, waiting for transfers between devices: 216 us -> 105 us  [the longest x4 98.5 us: sum_share(): lax.psum_scatter(partial.astype(LOW), 'tensor', scatter_dimension=0, tile...]
    all_gather x6 -> x9, waiting for transfers between devices: 89.8 us -> 174 us  [the longest x5 76.7 us: spread(): return lax.all_gather(share, 'tensor', axis=0, tiled=True)]
    all_gather x2 -> x1, blocking collectives: 63.9 us -> 18.7 us  [gather_rows(): mine = lax.all_gather(shard, 'dp', axis=0, tiled=False)]
    reduce_sum x12 -> x6, other arithmetic: 38.6 us -> 12 us  [row_sum(): return jnp.sum(values.reshape(-1, values.shape[-1]), axis=0)]
    unnamed x328 -> x141, local copies, waits for them, and re-layouts: 30.7 us -> 10.7 us
  transfers between devices with their start and end apart: 23 -> 28, of which waited for: 11 -> 19; matrix products, arithmetic and copies ran while one was open for 23% -> 17% of each run, Pallas kernels for 0% -> 0%
where the time goes in v1:
time: 895 us; the launch traced here: 890 us
  waiting for transfers between devices  516 us (58%)
  matrix products  128 us (14%)
  local copies, waits for them, and re-layouts  78.6 us (9%)
  other arithmetic  76.1 us (9%)
  blocking collectives  59.4 us (7%)
  starting transfers between devices  16.1 us (2%)
  between operations  15.6 us (2%)
    ppermute x10, waiting for transfers between devices, swap(): return lax.ppermute(values, 'seq', [(0, 1), (1, 0)])  236 us
    dot_general x24, matrix products, product(): return jnp.einsum(pattern, left_m, right_m, preferred_element_type=F32)  128 us
    reduce_scatter x4, waiting for transfers between devices, sum_share(): lax.psum_scatter(partial.astype(LOW), 'tensor', scatter_dimension=0, tile...  98.5 us
    all_gather x5, waiting for transfers between devices, spread(): return lax.all_gather(share, 'tensor', axis=0, tiled=True)  76.7 us
    all_gather x3, waiting for transfers between devices, gather_rows(): mine = lax.all_gather(shard, 'dp', axis=0, tiled=False)  75 us
    unnamed x1, blocking collectives  40.7 us
    all_gather x1, waiting for transfers between devices, body(): lax.all_gather(jnp.concatenate([kv_weight, gain_row], axis=0), ALL, axis=...  22.6 us
    convert_element_type x3, local copies, waits for them, and re-layouts, scatter_rows(): total = total.astype(LOW)  19.3 us
  transfers between devices with their start and end apart: 28, of which 19 were waited for; matrix products, arithmetic and copies ran while one was open for 17% of the time, Pallas kernels for 0%

profile of v1, /device:TPU:0, one launch (start us, length us, event | category | flops | bytes accessed | tf_op | source)
XLA Modules:
  0.0 890.2 jit_solution(4593842962445588083)
XLA Ops:
  7.2 4.1 concatenate.54
  13.8 18.7 %all-gather.1 = bf16[576,512]{1,0:T(8,128)(2,1)S(1)} all-gather(bf16[144,512]{1,0:T(8,128)(2,1)S(1)} %pad_maximum_fusion.11), channel_id=3, replica_groups=mesh['dp'=4,'seq'=2,'tensor'=4] {'dp'}, dimensions={0}, use_global_device_ids=true | all-gather | bytes 737280 | tf_op jit(solution)/shard_map/all_gather | solution.py:69
  37.0 9.2 %collective-permute-done = bf16[4,144,512]{2,1,0:T(8,128)(2,1)S(1)} collective-permute-done((bf16[4,144,512]{2,1,0:T(8,128)(2,1)S(1)}, bf16[4,144,512]{2,1,0:T(8,128)(2,1)S(1)}, u32[]{:S(2)}, u32[]{:S(2)}) %collective-permute-start) | collective-permute-done | bytes 589856 | tf_op jit(solution)/shard_map/ppermute | solution.py:55
  47.5 22.6 %all-gather.32.cloned.1.call-done = bf16[32,37,512]{2,1,0:T(8,128)(2,1)} async-done(((bf16[1,37,512]{2,1,0:T(8,128)(2,1)}), bf16[32,37,512]{2,1,0:T(8,128)(2,1)}) %all-gather.32.cloned.1.call-update) | async-done | bytes 1212432 | tf_op jit(solution)/shard_map/all_gather | solution.py:138
  71.5 2.9 reshape.314
  74.4 3.0 fusion.59
  79.2 3.2 fusion.96
  86.2 22.9 %collective-permute-done.1 = bf16[2,512,512]{1,2,0:T(8,128)(2,1)} collective-permute-done((bf16[2,512,512]{1,2,0:T(8,128)(2,1)}, bf16[2,512,512]{1,2,0:T(8,128)(2,1)}, u32[]{:S(2)}, u32[]{:S(2)}) %collective-permute-start.1) | collective-permute-done | bytes 1048608 | tf_op jit(solution)/shard_map/ppermute | solution.py:55
  112.2 4.2 copy.80
  128.2 33.3 %all-gather.26.cloned.1.call-done = bf16[576,1728]{1,0:T(8,128)(2,1)} async-done(((bf16[144,1728]{1,0:T(8,128)(2,1)}), bf16[576,1728]{1,0:T(8,128)(2,1)}) %all-gather.26.cloned.1.call-update) | async-done | bytes 1990672 | tf_op jit(solution)/shard_map/all_gather | solution.py:69
  163.0 33.3 %reduce-scatter.10.cloned.1.call-done = bf16[256,1152]{1,0:T(8,128)(2,1)} async-done(((bf16[1024,1152]{1,0:T(8,128)(2,1)}), bf16[256,1152]{1,0:T(8,128)(2,1)}) %reduce-scatter.10.cloned.1.call-update) | async-done | bytes 589840 | tf_op jit(solution)/shard_map/reduce_scatter | solution.py:92
  201.4 41.7 %all-gather.30.cloned.1.call-done = bf16[576,1728]{1,0:T(8,128)(2,1)} async-done(((bf16[144,1728]{1,0:T(8,128)(2,1)}), bf16[576,1728]{1,0:T(8,128)(2,1)}) %all-gather.30.cloned.1.call-update) | async-done | bytes 1990672 | tf_op jit(solution)/shard_map/all_gather | solution.py:69
  244.6 3.7 select_bitcast_fusion.3
  253.6 36.4 %collective-permute-done.4 = bf16[4,144,1728]{2,1,0:T(8,128)(2,1)S(1)} collective-permute-done((bf16[4,144,1728]{2,1,0:T(8,128)(2,1)}, bf16[4,144,1728]{2,1,0:T(8,128)(2,1)S(1)}, u32[]{:S(2)}, u32[]{:S(2)}) %collective-permute-start.4) | collective-permute-done | bytes 1990688 | tf_op jit(solution)/shard_map/ppermute | solution.py:55
  292.7 8.0 fusion.119
  300.8 19.9 %multiply_convert_fusion.1 = (bf16[1024,1728]{0,1:T(8,128)(2,1)}, f32[1024,1728]{0,1:T(8,128)}) fusion(f32[1024,1728]{0,1:T(8,128)S(1)} %fusion.119, bf16[1024,1152]{1,0:T(8,128)(2,1)S(1)} %copy-done.66, bf16[1152,1728]{1,0:T(8,128)(2,1)S(1)} %bitcast.181), kind=kOutput, calls=%fused_computation.14 | convolution fusion | flops 4094558208 | bytes 24035328 | tf_op jit(solution)/shard_map/rd,df->rf/dot_general | solution.py:47
  320.7 8.5 convolution_convert_fusion.3
  329.4 32.0 %reduce-scatter.12.cloned.1.call-done = bf16[256,1152]{1,0:T(8,128)(2,1)} async-done(((bf16[1024,1152]{1,0:T(8,128)(2,1)}), bf16[256,1152]{1,0:T(8,128)(2,1)}) %reduce-scatter.12.cloned.1.call-update) | async-done | bytes 589840 | tf_op jit(solution)/shard_map/reduce_scatter | solution.py:92
  367.5 24.2 %all-gather.20.cloned.1.call-done = bf16[1024,1152]{1,0:T(8,128)(2,1)} async-done(((bf16[256,1152]{1,0:T(8,128)(2,1)}), bf16[1024,1152]{1,0:T(8,128)(2,1)}) %all-gather.20.cloned.1.call-update) | async-done | bytes 2359312 | tf_op jit(solution)/shard_map/all_gather | solution.py:98
  391.7 17.6 %multiply_convert_fusion = (bf16[1024,1728]{0,1:T(8,128)(2,1)}, bf16[1024,1728]{0,1:T(8,128)(2,1)}) fusion(f32[1024,1728]{0,1:T(8,128)} %copy-done.67, f32[1024,1728]{0,1:T(8,128)} %get-tuple-element.70, bf16[1024,1152]{1,0:T(8,128)(2,1)} %all-gather.20.cloned.1.call-done, bf16[1152,1728]{1,0:T(8,128)(2,1)} %bitcast.185), kind=kOutput, calls=%fused_computation.13 | convolution fusion | flops 4119330816 | bytes 27574272 | tf_op jit(solution)/shard_map/rd,df->rf/dot_general | solution.py:47
  409.3 7.2 fusion.120
  416.5 6.5 add_convert_fusion
  423.1 33.2 %reduce-scatter.14.cloned.1.call-done = bf16[256,1152]{1,0:T(8,128)(2,1)} async-done(((bf16[1024,1152]{1,0:T(8,128)(2,1)}), bf16[256,1152]{1,0:T(8,128)(2,1)}) %reduce-scatter.14.cloned.1.call-update) | async-done | bytes 589840 | tf_op jit(solution)/shard_map/reduce_scatter | solution.py:92
  458.7 3.8 fusion.48
  464.7 24.2 %all-gather.22.cloned.1.call-done = bf16[1024,1152]{1,0:T(8,128)(2,1)} async-done(((bf16[256,1152]{1,0:T(8,128)(2,1)}), bf16[1024,1152]{1,0:T(8,128)(2,1)}) %all-gather.22.cloned.1.call-update) | async-done | bytes 2359312 | tf_op jit(solution)/shard_map/all_gather | solution.py:98
  499.5 4.1 multiply_convert_fusion.2
  514.3 21.5 %collective-permute-done.5 = bf16[2,512,512]{1,2,0:T(8,128)(2,1)} collective-permute-done((bf16[2,512,512]{1,2,0:T(8,128)(2,1)}, bf16[2,512,512]{1,2,0:T(8,128)(2,1)}, u32[]{:S(2)}, u32[]{:S(2)}) %collective-permute-start.5) | collective-permute-done | bytes 1048608 | tf_op jit(solution)/shard_map/ppermute | solution.py:55
  544.3 2.9 reshape.324
  547.2 3.0 copy.99
  550.3 2.9 reshape.355
  559.0 3.0 fusion.14
  562.2 9.5 %convolution_convert_fusion.2 = bf16[1152,1728]{0,1:T(8,128)(2,1)} fusion(bf16[1024,1728]{0,1:T(8,128)(2,1)} %get-tuple-element.29, bf16[1024,1152]{1,0:T(8,128)(2,1)} %all-gather.16.cloned.1.call-done), kind=kOutput, calls=%fused_computation.5 | convolution fusion | flops 4078854144 | bytes 9879552 | tf_op jit(solution)/shard_map/rd,rf->df/dot_general | solution.py:47
  571.7 6.4 copy.101
  581.4 44.8 %collective-permute-done.7 = bf16[4,144,1728]{2,1,0:T(8,128)(2,1)S(1)} collective-permute-done((bf16[4,144,1728]{2,1,0:T(8,128)(2,1)S(1)}, bf16[4,144,1728]{2,1,0:T(8,128)(2,1)S(1)}, u32[]{:S(2)}, u32[]{:S(2)}) %collective-permute-start.7) | collective-permute-done | bytes 1990688 | tf_op jit(solution)/shard_map/ppermute | solution.py:55
  628.0 9.5 %convolution_convert_fusion.1 = bf16[1152,1728]{0,1:T(8,128)(2,1)} fusion(bf16[1024,1728]{0,1:T(8,128)(2,1)} %get-tuple-element.28, bf16[1024,1152]{1,0:T(8,128)(2,1)} %all-gather.16.cloned.1.call-done), kind=kOutput, calls=%fused_computation.4 | convolution fusion | flops 4078854144 | bytes 9879552 | tf_op jit(solution)/shard_map/rd,rf->df/dot_general | solution.py:47
  637.5 6.4 copy.102
  647.2 43.9 %collective-permute-done.8 = bf16[4,144,1728]{2,1,0:T(8,128)(2,1)S(1)} collective-permute-done((bf16[4,144,1728]{2,1,0:T(8,128)(2,1)S(1)}, bf16[4,144,1728]{2,1,0:T(8,128)(2,1)S(1)}, u32[]{:S(2)}, u32[]{:S(2)}) %collective-permute-start.8) | collective-permute-done | bytes 1990688 | tf_op jit(solution)/shard_map/ppermute | solution.py:55
  693.2 9.5 %convolution_convert_fusion = bf16[1152,1728]{0,1:T(8,128)(2,1)} fusion(bf16[1024,1728]{0,1:T(8,128)(2,1)} %get-tuple-element.69, bf16[1024,1152]{1,0:T(8,128)(2,1)} %all-gather.20.cloned.1.call-done), kind=kOutput, calls=%fused_computation.3 | convolution fusion | flops 4078854144 | bytes 9879552 | tf_op jit(solution)/shard_map/rd,rf->df/dot_general | solution.py:47
  702.6 6.4 copy.103
  712.4 42.9 %collective-permute-done.9 = bf16[4,144,1728]{2,1,0:T(8,128)(2,1)S(1)} collective-permute-done((bf16[4,144,1728]{2,1,0:T(8,128)(2,1)S(1)}, bf16[4,144,1728]{2,1,0:T(8,128)(2,1)S(1)}, u32[]{:S(2)}, u32[]{:S(2)}) %collective-permute-start.9) | collective-permute-done | bytes 1990688 | tf_op jit(solution)/shard_map/ppermute | solution.py:55
  758.4 4.3 copy.96
  762.7 2.8 convolution_convert_fusion.7
  770.4 14.3 %collective-permute-done.6 = bf16[4,192,512]{2,1,0:T(8,128)(2,1)S(1)} collective-permute-done((bf16[4,192,512]{2,1,0:T(8,128)(2,1)S(1)}, bf16[4,192,512]{2,1,0:T(8,128)(2,1)S(1)}, u32[]{:S(2)}, u32[]{:S(2)}) %collective-permute-start.6) | collective-permute-done | bytes 786464 | tf_op jit(solution)/shard_map/ppermute | solution.py:55
  794.7 6.2 reduce-scatter.26.cloned.1.call-done
  802.9 22.7 %all-gather.18.cloned.1.call-done = bf16[1024,1152]{1,0:T(8,128)(2,1)} async-done(((bf16[256,1152]{1,0:T(8,128)(2,1)}), bf16[1024,1152]{1,0:T(8,128)(2,1)}) %all-gather.18.cloned.1.call-update) | async-done | bytes 2359312 | tf_op jit(solution)/shard_map/all_gather | solution.py:98
  826.1 40.7 %all-reduce.1 = f32[32,160]{1,0:T(8,128)S(1)} all-reduce(f32[32,160]{1,0:T(8,128)S(1)} %concatenate.69), channel_id=16, replica_groups=mesh['dp'=4,'seq'=2,'tensor'=4] {'dp','seq','tensor'}, use_global_device_ids=true, to_apply=%region_31.32.clone | all-reduce | flops 5120 | bytes 40960
  872.6 5.7 all-gather.24.cloned.1.call-done
  878.3 3.4 copy.126
  (302 shorter events, 133.5 us)
Async XLA Ops:
  7.2 62.9 %all-gather.32.cloned.1.call-start = ((), (), s32[]{:S(2)}) async-start(), calls=%async_computation.26 | async-start | bytes 1351680 | tf_op jit(solution)/shard_map/all_gather | solution.py:138
  12.8 113.9 %all-gather.28.cloned.1.call-start = ((), (), s32[]{:S(2)}) async-start(), calls=%async_computation.24 | async-start | bytes 2580480 | tf_op jit(solution)/shard_map/all_gather | solution.py:69
  32.5 13.7 %collective-permute-start = (bf16[4,144,512]{2,1,0:T(8,128)(2,1)S(1)}, bf16[4,144,512]{2,1,0:T(8,128)(2,1)S(1)}, u32[]{:S(2)}, u32[]{:S(2)}) collective-permute-start(bf16[4,144,512]{2,1,0:T(8,128)(2,1)S(1)} %bitcast.188), channel_id=1, source_target_pairs={{0,4},{4,0},{1,5},{5,1},{2,6},{6,2},{3,7},{7,3},{8,12},{12,8},{9,1... | collective-permute-start | bytes 1769480 | tf_op jit(solution)/shard_map/ppermute | solution.py:55
  34.0 127.5 %all-gather.26.cloned.1.call-start = ((), (), s32[]{:S(2)}) async-start(), calls=%async_computation.23 | async-start | bytes 2580480 | tf_op jit(solution)/shard_map/all_gather | solution.py:69
  34.8 44.4 %copy-start.45 = (f32[2,512]{1,0:T(2,128)}, f32[2,512]{1,0:T(2,128)S(1)}, u32[]{:S(2)}) copy-start(f32[2,512]{1,0:T(2,128)S(1)} %convert_element_type.184) | copy-start | bytes 12292
  34.8 44.4 %copy-start.64 = (f32[128]{0:T(128)}, f32[128]{0:T(128)S(1)}, u32[]{:S(2)}) copy-start(f32[128]{0:T(128)S(1)} %negate_power_fusion) | copy-start | bytes 1540
  37.0 40.7 %copy-start.61 = (f32[2,512]{1,0:T(2,128)}, f32[2,512]{1,0:T(2,128)S(1)}, u32[]{:S(2)}) copy-start(f32[2,512]{1,0:T(2,128)S(1)} %add_rsqrt_fusion.2) | copy-start | bytes 12292
  46.4 28.0 %copy-start.6 = (bf16[2,512,1152]{2,1,0:T(8,128)(2,1)S(1)}, bf16[2,512,1152]{2,1,0:T(8,128)(2,1)}, u32[]{:S(2)}) copy-start(bf16[2,512,1152]{2,1,0:T(8,128)(2,1)} %param.15) | copy-start | bytes 7077892
  83.4 25.7 %collective-permute-start.1 = (bf16[2,512,512]{1,2,0:T(8,128)(2,1)}, bf16[2,512,512]{1,2,0:T(8,128)(2,1)}, u32[]{:S(2)}, u32[]{:S(2)}) collective-permute-start(bf16[2,512,512]{1,2,0:T(8,128)(2,1)} %pad_maximum_fusion.5), channel_id=1, source_target_pairs={{0,4},{4,0},{1,5},{5,1},{2,6},{6,2},{3,7},{7,3},{8,12},{12,8},{9,1... | collective-permute-start | bytes 3145736 | tf_op jit(solution)/shard_map/ppermute | solution.py:55
  85.0 111.3 %reduce-scatter.10.cloned.1.call-start = ((), (), s32[]{:S(2)}) async-start(), calls=%async_computation.9 | async-start | bytes 2949120 | tf_op jit(solution)/shard_map/reduce_scatter | solution.py:92
  125.6 117.6 %all-gather.30.cloned.1.call-start = ((), (), s32[]{:S(2)}) async-start(), calls=%async_computation.25 | async-start | bytes 2580480 | tf_op jit(solution)/shard_map/all_gather | solution.py:69
  126.1 166.6 %all-gather.16.cloned.1.call-start = ((), (), s32[]{:S(2)}) async-start(), calls=%async_computation.10 | async-start | bytes 2949120 | tf_op jit(solution)/shard_map/all_gather | solution.py:98
  126.7 117.9 %collective-permute-start.3 = (bf16[4,144,1728]{2,1,0:T(8,128)(2,1)}, bf16[4,144,1728]{2,1,0:T(8,128)(2,1)}, u32[]{:S(2)}, u32[]{:S(2)}) collective-permute-start(bf16[4,144,1728]{2,1,0:T(8,128)(2,1)} %bitcast.194), channel_id=1, source_target_pairs={{0,4},{4,0},{1,5},{5,1},{2,6},{6,2},{3,7},{7,3},{8,12},{12,8},{9,1... | collective-permute-start | bytes 5971976 | tf_op jit(solution)/shard_map/ppermute | solution.py:55
  161.5 83.1 %collective-permute-start.2 = (bf16[4,144,1728]{2,1,0:T(8,128)(2,1)}, bf16[4,144,1728]{2,1,0:T(8,128)(2,1)}, u32[]{:S(2)}, u32[]{:S(2)}) collective-permute-start(bf16[4,144,1728]{2,1,0:T(8,128)(2,1)} %bitcast.196), channel_id=1, source_target_pairs={{0,4},{4,0},{1,5},{5,1},{2,6},{6,2},{3,7},{7,3},{8,12},{12,8},{9,1... | collective-permute-start | bytes 5971976 | tf_op jit(solution)/shard_map/ppermute | solution.py:55
  197.6 50.7 %copy-start.47 = (f32[256]{0:T(256)}, f32[256]{0:T(256)S(1)}, u32[]{:S(2)}) copy-start(f32[256]{0:T(256)S(1)} %add_rsqrt_fusion.6) | copy-start | bytes 3076
  199.1 49.2 %copy-start.54 = (f32[256]{0:T(256)}, f32[256]{0:T(256)S(1)}, u32[]{:S(2)}) copy-start(f32[256]{0:T(256)S(1)} %add_rsqrt_fusion.5) | copy-start | bytes 3076
  201.4 160.0 %reduce-scatter.12.cloned.1.call-start = ((), (), s32[]{:S(2)}) async-start(), calls=%async_computation.11 | async-start | bytes 2949120 | tf_op jit(solution)/shard_map/reduce_scatter | solution.py:92
  243.1 46.9 %collective-permute-start.4 = (bf16[4,144,1728]{2,1,0:T(8,128)(2,1)}, bf16[4,144,1728]{2,1,0:T(8,128)(2,1)S(1)}, u32[]{:S(2)}, u32[]{:S(2)}) collective-permute-start(bf16[4,144,1728]{2,1,0:T(8,128)(2,1)} %bitcast.198), channel_id=1, source_target_pairs={{0,4},{4,0},{1,5},{5,1},{2,6},{6,2},{3,7},{7,3},{8,12},{12,8},{9,1... | collective-permute-start | bytes 5971976 | tf_op jit(solution)/shard_map/ppermute | solution.py:55
  251.3 38.7 %copy-start.35 = (bf16[576,1728]{1,0:T(8,128)(2,1)S(1)}, bf16[576,1728]{1,0:T(8,128)(2,1)}, u32[]{:S(2)}) copy-start(bf16[576,1728]{1,0:T(8,128)(2,1)} %all-gather.30.cloned.1.call-done) | copy-start | bytes 5971972
  300.7 20.0 %copy-start.67 = (f32[1024,1728]{0,1:T(8,128)}, f32[1024,1728]{0,1:T(8,128)S(1)}, u32[]{:S(2)}) copy-start(f32[1024,1728]{0,1:T(8,128)S(1)} %fusion.119) | copy-start | bytes 21233668
  300.8 20.0 %copy-start.21 = (bf16[4,2,144,1728]{3,2,1,0:T(8,128)(2,1)S(1)}, bf16[4,2,144,1728]{3,2,1,0:T(8,128)(2,1)}, u32[]{:S(2)}) copy-start(bf16[4,2,144,1728]{3,2,1,0:T(8,128)(2,1)} %pad_maximum_fusion.2) | copy-start | bytes 11943940
  329.2 62.4 %all-gather.20.cloned.1.call-start = ((), (), s32[]{:S(2)}) async-start(), calls=%async_computation.13 | async-start | bytes 2949120 | tf_op jit(solution)/shard_map/all_gather | solution.py:98
  329.4 79.9 %copy-start.38 = (f32[1152]{0:T(1024)}, f32[1152]{0:T(1024)S(1)}, u32[]{:S(2)}) copy-start(f32[1152]{0:T(1024)S(1)} %add.253) | copy-start | bytes 13828
  362.7 46.6 %copy-start.55 = (f32[256]{0:T(256)}, f32[256]{0:T(256)S(1)}, u32[]{:S(2)}) copy-start(f32[256]{0:T(256)S(1)} %add_rsqrt_fusion.4) | copy-start | bytes 3076
  367.4 88.8 %reduce-scatter.14.cloned.1.call-start = ((), (), s32[]{:S(2)}) async-start(), calls=%async_computation.14 | async-start | bytes 2949120 | tf_op jit(solution)/shard_map/reduce_scatter | solution.py:92
  391.7 17.6 %copy-start.20 = (bf16[4,2,144,1728]{3,2,1,0:T(8,128)(2,1)S(1)}, bf16[4,2,144,1728]{3,2,1,0:T(8,128)(2,1)}, u32[]{:S(2)}) copy-start(bf16[4,2,144,1728]{3,2,1,0:T(8,128)(2,1)} %copy.82) | copy-start | bytes 11943940
  423.0 33.2 %copy-start = (bf16[256,1152]{1,0:T(8,128)(2,1)S(1)}, bf16[256,1152]{1,0:T(8,128)(2,1)}, u32[]{:S(2)}) copy-start(bf16[256,1152]{1,0:T(8,128)(2,1)} %reduce-scatter.10.cloned.1.call-done) | copy-start | bytes 1769476
  423.0 35.6 %copy-start.10 = (bf16[256,1152]{1,0:T(8,128)(2,1)S(1)}, bf16[256,1152]{1,0:T(8,128)(2,1)}, u32[]{:S(2)}) copy-start(bf16[256,1152]{1,0:T(8,128)(2,1)} %reduce-scatter.12.cloned.1.call-done) | copy-start | bytes 1769476
  423.0 65.8 %all-gather.22.cloned.1.call-start = ((), (), s32[]{:S(2)}) async-start(), calls=%async_computation.15 | async-start | bytes 2949120 | tf_op jit(solution)/shard_map/all_gather | solution.py:98
  464.6 302.0 %reduce-scatter.18.cloned.1.call-start = ((), (), s32[]{:S(2)}) async-start(), calls=%async_computation.18 | async-start | bytes 1474560 | tf_op jit(solution)/shard_map/reduce_scatter | solution.py:252
  464.7 26.9 %copy-start.53 = (f32[2,512]{1,0:T(2,128)S(1)}, f32[2,512]{1,0:T(2,128)}, u32[]{:S(2)}) copy-start(f32[2,512]{1,0:T(2,128)} %copy-done.52) | copy-start | bytes 12292
  510.2 25.6 %collective-permute-start.5 = (bf16[2,512,512]{1,2,0:T(8,128)(2,1)}, bf16[2,512,512]{1,2,0:T(8,128)(2,1)}, u32[]{:S(2)}, u32[]{:S(2)}) collective-permute-start(bf16[2,512,512]{1,2,0:T(8,128)(2,1)} %fusion.62), channel_id=1, source_target_pairs={{0,4},{4,0},{1,5},{5,1},{2,6},{6,2},{3,7},{7,3},{8,12},{12,8},{9,1... | collective-permute-start | bytes 3145736 | tf_op jit(solution)/shard_map/ppermute | solution.py:55
  514.3 23.4 %copy-start.46 = (f32[2,512]{1,0:T(2,128)S(1)}, f32[2,512]{1,0:T(2,128)}, u32[]{:S(2)}) copy-start(f32[2,512]{1,0:T(2,128)} %copy-done.45) | copy-start | bytes 12292
  514.3 23.4 %copy-start.65 = (f32[128]{0:T(128)S(1)}, f32[128]{0:T(128)}, u32[]{:S(2)}) copy-start(f32[128]{0:T(128)} %copy-done.64) | copy-start | bytes 1540
  550.3 235.7 %reduce-scatter.16.cloned.1.call-start = ((), (), s32[]{:S(2)}) async-start(), calls=%async_computation.16 | async-start | bytes 2949120 | tf_op jit(solution)/shard_map/reduce_scatter | solution.py:92
  562.0 228.6 %reduce-scatter.22.cloned.1.call-start = ((), (), s32[]{:S(2)}) async-start(), calls=%async_computation.20 | async-start | bytes 2580480 | tf_op jit(solution)/shard_map/reduce_scatter | solution.py:88
  578.1 48.0 %copy-start.3 = (bf16[1152,1728]{1,0:T(8,128)(2,1)S(1)}, bf16[1152,1728]{1,0:T(8,128)(2,1)}, u32[]{:S(2)}) copy-start(bf16[1152,1728]{1,0:T(8,128)(2,1)} %copy.101) | copy-start | bytes 11943940
  580.0 46.2 %collective-permute-start.7 = (bf16[4,144,1728]{2,1,0:T(8,128)(2,1)S(1)}, bf16[4,144,1728]{2,1,0:T(8,128)(2,1)S(1)}, u32[]{:S(2)}, u32[]{:S(2)}) collective-permute-start(bf16[4,144,1728]{2,1,0:T(8,128)(2,1)S(1)} %dynamic-slice_bitcast_fusion.2), channel_id=1, source_target_pairs={{0,4},{4,0},{1,5},{5,1},{2,6},{6,2},{3,7},{7,3},{8,12},{12,8},{9,1... | collective-permute-start | bytes 5971976 | tf_op jit(solution)/shard_map/ppermute | solution.py:55
  628.0 164.7 %reduce-scatter.24.cloned.1.call-start = ((), (), s32[]{:S(2)}) async-start(), calls=%async_computation.21 | async-start | bytes 2580480 | tf_op jit(solution)/shard_map/reduce_scatter | solution.py:88
  643.9 47.2 %copy-start.4 = (bf16[1152,1728]{1,0:T(8,128)(2,1)S(1)}, bf16[1152,1728]{1,0:T(8,128)(2,1)}, u32[]{:S(2)}) copy-start(bf16[1152,1728]{1,0:T(8,128)(2,1)} %copy.102) | copy-start | bytes 11943940
  645.8 45.3 %collective-permute-start.8 = (bf16[4,144,1728]{2,1,0:T(8,128)(2,1)S(1)}, bf16[4,144,1728]{2,1,0:T(8,128)(2,1)S(1)}, u32[]{:S(2)}, u32[]{:S(2)}) collective-permute-start(bf16[4,144,1728]{2,1,0:T(8,128)(2,1)S(1)} %dynamic-slice_bitcast_fusion.1), channel_id=1, source_target_pairs={{0,4},{4,0},{1,5},{5,1},{2,6},{6,2},{3,7},{7,3},{8,12},{12,8},{9,1... | collective-permute-start | bytes 5971976 | tf_op jit(solution)/shard_map/ppermute | solution.py:55
  692.9 108.0 %reduce-scatter.26.cloned.1.call-start = ((), (), s32[]{:S(2)}) async-start(), calls=%async_computation.22 | async-start | bytes 2580480 | tf_op jit(solution)/shard_map/reduce_scatter | solution.py:88
  709.1 46.3 %copy-start.5 = (bf16[1152,1728]{1,0:T(8,128)(2,1)S(1)}, bf16[1152,1728]{1,0:T(8,128)(2,1)}, u32[]{:S(2)}) copy-start(bf16[1152,1728]{1,0:T(8,128)(2,1)} %copy.103) | copy-start | bytes 11943940
  710.9 44.4 %collective-permute-start.9 = (bf16[4,144,1728]{2,1,0:T(8,128)(2,1)S(1)}, bf16[4,144,1728]{2,1,0:T(8,128)(2,1)S(1)}, u32[]{:S(2)}, u32[]{:S(2)}) collective-permute-start(bf16[4,144,1728]{2,1,0:T(8,128)(2,1)S(1)} %dynamic-slice_bitcast_fusion), channel_id=1, source_target_pairs={{0,4},{4,0},{1,5},{5,1},{2,6},{6,2},{3,7},{7,3},{8,12},{12,8},{9,1... | collective-permute-start | bytes 5971976 | tf_op jit(solution)/shard_map/ppermute | solution.py:55
  757.2 68.5 %all-gather.18.cloned.1.call-start = ((), (), s32[]{:S(2)}) async-start(), calls=%async_computation.12 | async-start | bytes 2949120 | tf_op jit(solution)/shard_map/all_gather | solution.py:98
  757.7 110.2 %reduce-scatter.20.cloned.1.call-start = ((), (), s32[]{:S(2)}) async-start(), calls=%async_computation.19 | async-start | bytes 983040 | tf_op jit(solution)/shard_map/reduce_scatter | solution.py:88
  768.9 15.8 %collective-permute-start.6 = (bf16[4,192,512]{2,1,0:T(8,128)(2,1)S(1)}, bf16[4,192,512]{2,1,0:T(8,128)(2,1)S(1)}, u32[]{:S(2)}, u32[]{:S(2)}) collective-permute-start(bf16[4,192,512]{2,1,0:T(8,128)(2,1)S(1)} %dynamic-slice_bitcast_fusion.3), channel_id=1, source_target_pairs={{0,4},{4,0},{1,5},{5,1},{2,6},{6,2},{3,7},{7,3},{8,12},{12,8},{9,1... | collective-permute-start | bytes 2359304 | tf_op jit(solution)/shard_map/ppermute | solution.py:55
  785.8 92.5 %all-gather.24.cloned.1.call-start = ((), (), s32[]{:S(2)}) async-start(), calls=%async_computation.17 | async-start | bytes 2949120 | tf_op jit(solution)/shard_map/all_gather | solution.py:98
  (49 other events, 181.6 us)
Sparse Core Ops, SparseCore 0:
  12.9 57.1 all-gather.31
  71.6 44.2 all-gather.27
  117.5 43.9 all-gather.25
  164.5 31.7 reduce-scatter.9
  197.8 45.2 all-gather.29
  245.2 22.7 all-gather.15
  329.3 31.9 reduce-scatter.11
  367.6 24.0 all-gather.19
  423.2 33.0 reduce-scatter.13
  464.7 24.0 all-gather.21
  550.4 25.7 reduce-scatter.17
  579.1 33.0 reduce-scatter.15
  628.1 43.0 reduce-scatter.21
  693.0 43.2 reduce-scatter.23
  757.3 43.5 reduce-scatter.25
  802.3 23.3 all-gather.17
  828.4 23.7 reduce-scatter.19
  854.2 24.0 all-gather.23

commit v2 on v1

--- a/solution.py
+++ b/solution.py
@@ -71,9 +71,20 @@
     return both.reshape(-1, shard.shape[-1])
 
 
+def add_dp(pair):
+    dp_n = lax.axis_size("dp")
+    me = lax.axis_index("dp")
+    total = lax.dynamic_index_in_dim(pair, me, 0, keepdims=False).astype(F32)
+    for step in range(1, dp_n):
+        sent = lax.dynamic_index_in_dim(pair, lax.rem(me + step, dp_n), 0, keepdims=False)
+        total = total + lax.ppermute(
+            sent, "dp", [(index, (index + step) % dp_n) for index in range(dp_n)]
+        ).astype(F32)
+    return total
+
+
 def scatter_rows(total):
     seq_n = lax.axis_size("seq")
-    total = total.astype(LOW)
     if seq_n != 2:
         return lax.psum_scatter(
             total, ("dp", "seq"), scatter_dimension=0, tiled=True
@@ -83,19 +94,42 @@
     parts = total.reshape(dp_n, 2, -1, total.shape[-1])
     away = lax.dynamic_index_in_dim(parts, 1 - me, 1, keepdims=False)
     stay = lax.dynamic_index_in_dim(parts, me, 1, keepdims=False)
-    pair = (stay.astype(F32) + swap(away).astype(F32)).astype(LOW)
-    pair = pair.reshape(-1, total.shape[-1])
-    return lax.psum_scatter(pair, "dp", scatter_dimension=0, tiled=True).astype(F32)
+    return add_dp((stay.astype(F32) + swap(away).astype(F32)).astype(LOW))
+
+
+def across(values, bit):
+    return lax.ppermute(values, "tensor", [(index, index ^ bit) for index in range(4)])
+
+
+def add_tensor(parts):
+    if lax.axis_size("tensor") != 4:
+        return lax.psum_scatter(parts, "tensor", scatter_dimension=0).astype(F32)
+    me = lax.axis_index("tensor")
+    low, high = lax.rem(me, 2), me // 2
+    pairs = parts.reshape((2, 2) + parts.shape[1:])
+    sent = lax.dynamic_index_in_dim(pairs, 1 - low, 1, keepdims=False)
+    kept = lax.dynamic_index_in_dim(pairs, low, 1, keepdims=False)
+    kept = (kept.astype(F32) + across(sent, 1).astype(F32)).astype(LOW)
+    sent = lax.dynamic_index_in_dim(kept, 1 - high, 0, keepdims=False)
+    kept = lax.dynamic_index_in_dim(kept, high, 0, keepdims=False)
+    return kept.astype(F32) + across(sent, 2).astype(F32)
 
 
 def sum_share(partial):
-    return lax.psum_scatter(
-        partial.astype(LOW), "tensor", scatter_dimension=0, tiled=True
-    ).astype(F32)
+    tensor_n = lax.axis_size("tensor")
+    return add_tensor(partial.astype(LOW).reshape(tensor_n, -1, partial.shape[-1]))
 
 
 def spread(share):
-    return lax.all_gather(share, "tensor", axis=0, tiled=True)
+    if lax.axis_size("tensor") != 4:
+        return lax.all_gather(share, "tensor", axis=0, tiled=True)
+    me = lax.axis_index("tensor")
+    even, first = lax.rem(me, 2) == 0, me // 2 == 0
+    other = across(share, 2)
+    both = jnp.stack([jnp.where(first, share, other), jnp.where(first, other, share)], axis=0)
+    other = across(both, 1)
+    full = jnp.stack([jnp.where(even, both, other), jnp.where(even, other, both)], axis=1)
+    return full.reshape(-1, share.shape[-1])
 
 
 def row_sum(values):
@@ -135,9 +169,10 @@
     )
     gain_n = gain_row.shape[0]
     gain_row = jnp.pad(gain_row, (0, 2 * head - gain_n))[None]
+    fill = jnp.zeros((-(part + 1) % 16, 2 * head), LOW)
     small = lax.all_gather(
-        jnp.concatenate([kv_weight, gain_row], axis=0), ALL, axis=0, tiled=False
-    )
+        jnp.concatenate([kv_weight, gain_row, fill], axis=0), ALL, axis=0, tiled=True
+    ).reshape(all_n, -1, 2 * head)
     kv_mat = small[:, :part].reshape(width, 2 * head)
     gains = small[:, part, :gain_n].astype(F32)
 
@@ -204,7 +239,9 @@
     d_ffn = spread(norm_back(ffn_hat, ffn_fac, back * scale_fo).astype(LOW))
     result = spread((middle + ffn_hat * scale_fo).astype(LOW)).reshape(tokens.shape)
 
-    g_down = scatter_rows(product("rd,rf->df", d_ffn, acted)).T
+    g_down = product("rd,rf->df", d_ffn, acted).astype(LOW)
+    d_ffn, g_down = lax.optimization_barrier((d_ffn, g_down))
+    g_down = scatter_rows(g_down).T
     d_acted = product("rd,df->rf", d_ffn, down_mat)
     unused_out, pull_back = jax.vjp(gelu_mix, gate_v, upper_v)
     d_gate, d_up = pull_back(d_acted)
@@ -213,8 +250,11 @@
     d_nffn = sum_share(
         product("rf,df->rd", d_gate, gate_mat) + product("rf,df->rd", d_up, up_mat)
     )
-    g_gate = scatter_rows(product("rd,rf->df", normed_ffn, d_gate))
-    g_up = scatter_rows(product("rd,rf->df", normed_ffn, d_up))
+    g_gate = product("rd,rf->df", normed_ffn, d_gate).astype(LOW)
+    g_up = product("rd,rf->df", normed_ffn, d_up).astype(LOW)
+    d_nffn, g_gate, g_up = lax.optimization_barrier((d_nffn, g_gate, g_up))
+    g_gate = scatter_rows(g_gate)
+    g_up = scatter_rows(g_up)
     g_fi = row_sum(d_nffn * mid_hat)
     d_middle = back + norm_back(mid_hat, mid_fac, d_nffn * scale_fi)
     g_ao = row_sum(d_middle * br_hat)
@@ -249,7 +289,8 @@
     d_normed = sum_share(d_normed.reshape(rows_n, width))
     g_kv = product("scd,sce->de", normed, d_kvraw).astype(LOW)
     g_kv = g_kv.reshape(blocks_n, tensor_n, part, 2 * head)
-    g_kv = lax.psum_scatter(g_kv, "tensor", scatter_dimension=1, tiled=False)
+    g_kv = add_tensor(jnp.swapaxes(g_kv, 0, 1).reshape(tensor_n, -1, 2 * head))
+    g_kv = g_kv.astype(LOW).reshape(blocks_n, part, 2 * head)
     g_qmat = product("scd,sce->de", normed, d_qraw)
     g_qo = jnp.concatenate([g_qmat, g_out], axis=1).astype(LOW)
     g_qo = g_qo.reshape(blocks_n, width // blocks_n, 2 * head)
@@ -263,7 +304,9 @@
     gain_terms = jnp.concatenate(
         [entry.reshape(all_n, -1) for entry in (g_ai, g_ao, g_fi, g_fo, g_q, g_k)], axis=1
     )
-    gain_sums = lax.psum_scatter(gain_terms, ALL, scatter_dimension=0, tiled=True)[0]
+    gain_all = lax.all_gather(gain_terms, ALL, axis=0, tiled=False)
+    own = lax.dynamic_index_in_dim(gain_all, lax.axis_index(ALL), 1, keepdims=False)
+    gain_sums = jnp.sum(own, axis=0)
     return (
         result,
         d_input,

time: 895 us -> 731 us (0.82)
  waiting for transfers between devices: 516 us -> 307 us
  starting transfers between devices: 16.1 us -> 56.9 us
  matrix products: 128 us -> 100 us
  local copies, waits for them, and re-layouts: 78.6 us -> 90.5 us
    ppermute x10, waiting for transfers between devices: 236 us -> 117 us  [swap(): return lax.ppermute(values, 'seq', [(0, 1), (1, 0)])]
    reduce_scatter x9 -> x0, waiting for transfers between devices: 105 us -> none  [the longest x4 98.5 us: sum_share(): lax.psum_scatter(partial.astype(LOW), 'tensor', scatter_dimension=0, tile...]
    ppermute x0 -> x32, waiting for transfers between devices: none -> 88.8 us  [the longest x20 66.6 us: across(): lax.ppermute(values, 'tensor', [(index, index ^ bit) for index in range(4)])]
    all_gather x6 -> x1, waiting for transfers between devices: 99.3 us -> 23.5 us  [body(): lax.all_gather(jnp.concatenate([kv_weight, gain_row, fill], axis=0), ALL,...]
    ppermute x0 -> x32, starting transfers between devices: none -> 47.3 us  [the longest x12 34.5 us: add_dp(): lax.ppermute(sent, 'dp', [(index, (index + step) % dp_n) for index in ran...]
    all_gather x0 -> x1, blocking collectives: none -> 45.2 us  [body(): gain_all = lax.all_gather(gain_terms, ALL, axis=0, tiled=False)]
    unnamed x1 -> x0, blocking collectives: 40.7 us -> none
    dot_general x24, matrix products: 128 us -> 100 us  [product(): return jnp.einsum(pattern, left_m, right_m, preferred_element_type=F32)]
  transfers between devices with their start and end apart: 28 -> 46, of which waited for: 19 -> 22; matrix products, arithmetic and copies ran while one was open for 17% -> 31% of each run, Pallas kernels for 0% -> 0%
where the time goes in v2:
time: 731 us; the launch traced here: 719 us
  waiting for transfers between devices  307 us (42%)
  matrix products  100 us (14%)
  local copies, waits for them, and re-layouts  90.5 us (12%)
  other arithmetic  84.5 us (12%)
  blocking collectives  64.1 us (9%)
  starting transfers between devices  56.9 us (8%)
  between operations  15.7 us (2%)
    ppermute x10, waiting for transfers between devices, swap(): return lax.ppermute(values, 'seq', [(0, 1), (1, 0)])  117 us
    dot_general x24, matrix products, product(): return jnp.einsum(pattern, left_m, right_m, preferred_element_type=F32)  100 us
    all_gather x3, waiting for transfers between devices, gather_rows(): mine = lax.all_gather(shard, 'dp', axis=0, tiled=False)  77 us
    ppermute x20, waiting for transfers between devices, across(): lax.ppermute(values, 'tensor', [(index, index ^ bit) for index in range(4)])  66.6 us
    all_gather x1, blocking collectives, body(): gain_all = lax.all_gather(gain_terms, ALL, axis=0, tiled=False)  45.2 us
    ppermute x12, starting transfers between devices, add_dp(): lax.ppermute(sent, 'dp', [(index, (index + step) % dp_n) for index in ran...  34.5 us
    all_gather x1, waiting for transfers between devices, body(): lax.all_gather(jnp.concatenate([kv_weight, gain_row, fill], axis=0), ALL,...  23.5 us
    ppermute x12, waiting for transfers between devices, add_dp(): lax.ppermute(sent, 'dp', [(index, (index + step) % dp_n) for index in ran...  22.2 us
  transfers between devices with their start and end apart: 46, of which 22 were waited for; matrix products, arithmetic and copies ran while one was open for 31% of the time, Pallas kernels for 0%

profile of v2, /device:TPU:0, one launch (start us, length us, event | category | flops | bytes accessed | tf_op | source)
XLA Modules:
  0.0 718.9 jit_solution(3844188458383570847)
XLA Ops:
  7.2 4.1 concatenate.54
  14.7 18.9 %all-gather = bf16[576,512]{1,0:T(8,128)(2,1)S(1)} all-gather(bf16[144,512]{1,0:T(8,128)(2,1)S(1)} %pad_maximum_fusion.21), channel_id=2, replica_groups=mesh['dp'=4,'seq'=2,'tensor'=4] {'dp'}, dimensions={0}, use_global_device_ids=true | all-gather | bytes 737280 | tf_op jit(solution)/shard_map/all_gather | solution.py:69
  37.4 9.7 %collective-permute-done = bf16[4,144,512]{2,1,0:T(8,128)(2,1)S(1)} collective-permute-done((bf16[4,144,512]{2,1,0:T(8,128)(2,1)S(1)}, bf16[4,144,512]{2,1,0:T(8,128)(2,1)S(1)}, u32[]{:S(2)}, u32[]{:S(2)}) %collective-permute-start) | collective-permute-done | bytes 589856 | tf_op jit(solution)/shard_map/ppermute | solution.py:55
  47.5 23.5 %all-gather.10.cloned.1.call-done = bf16[1536,512]{1,0:T(8,128)(2,1)} async-done(((bf16[48,512]{1,0:T(8,128)(2,1)}), bf16[1536,512]{1,0:T(8,128)(2,1)}) %all-gather.10.cloned.1.call-update) | async-done | bytes 1572880 | tf_op jit(solution)/shard_map/all_gather | solution.py:173
  75.7 3.8 fusion.44
  88.2 23.0 %collective-permute-done.1 = bf16[2,512,512]{1,2,0:T(8,128)(2,1)} collective-permute-done((bf16[2,512,512]{1,2,0:T(8,128)(2,1)}, bf16[2,512,512]{1,2,0:T(8,128)(2,1)}, u32[]{:S(2)}, u32[]{:S(2)}) %collective-permute-start.1) | collective-permute-done | bytes 1048608 | tf_op jit(solution)/shard_map/ppermute | solution.py:55
  122.7 2.9 collective-permute-done.2
  129.3 33.0 %all-gather.14.cloned.1.call-done = bf16[576,1728]{1,0:T(8,128)(2,1)} async-done(((bf16[144,1728]{1,0:T(8,128)(2,1)}), bf16[576,1728]{1,0:T(8,128)(2,1)}) %all-gather.14.cloned.1.call-update) | async-done | bytes 1990672 | tf_op jit(solution)/shard_map/all_gather | solution.py:69
  163.8 44.0 %all-gather.16.cloned.1.call-done = bf16[576,1728]{1,0:T(8,128)(2,1)} async-done(((bf16[144,1728]{1,0:T(8,128)(2,1)}), bf16[576,1728]{1,0:T(8,128)(2,1)}) %all-gather.16.cloned.1.call-update) | async-done | bytes 1990672 | tf_op jit(solution)/shard_map/all_gather | solution.py:69
  215.3 5.9 collective-permute-done.7
  221.2 2.8 select_bitcast_fusion.3
  224.4 4.3 collective-permute-done.4
  230.2 34.2 %collective-permute-done.8 = bf16[4,144,1728]{2,1,0:T(8,128)(2,1)} collective-permute-done((bf16[4,144,1728]{2,1,0:T(8,128)(2,1)}, bf16[4,144,1728]{2,1,0:T(8,128)(2,1)}, u32[]{:S(2)}, u32[]{:S(2)}) %collective-permute-start.8) | collective-permute-done | bytes 1990688 | tf_op jit(solution)/shard_map/ppermute | solution.py:55
  267.1 7.0 fusion.120
  274.1 10.6 %multiply_convert_fusion.1 = (bf16[1024,1728]{0,1:T(8,128)(2,1)S(1)}, f32[1024,1728]{0,1:T(8,128)}) fusion(f32[1024,1728]{0,1:T(8,128)} %fusion.120, bf16[1024,1152]{1,0:T(8,128)(2,1)S(1)} %bitcast.328, bf16[1152,1728]{1,0:T(8,128)(2,1)S(1)} %bitcast.320), kind=kOutput, calls=%fused_computation.14 | convolution fusion | flops 4094558208 | bytes 24035328 | tf_op jit(solution)/shard_map/rd,df->rf/dot_general | solution.py:47
  284.7 5.5 convolution_convert_fusion.3
  290.4 2.8 collective-permute-done.9
  296.4 13.7 %collective-permute-done.10 = bf16[256,1152]{1,0:T(8,128)(2,1)} collective-permute-done((bf16[256,1152]{1,0:T(8,128)(2,1)}, bf16[256,1152]{1,0:T(8,128)(2,1)}, u32[]{:S(2)}, u32[]{:S(2)}) %collective-permute-start.10) | collective-permute-done | bytes 589856 | tf_op jit(solution)/shard_map/ppermute | solution.py:101
  318.5 14.2 %collective-permute-done.13 = bf16[256,1152]{1,0:T(8,128)(2,1)S(1)} collective-permute-done((bf16[256,1152]{1,0:T(8,128)(2,1)S(1)}, bf16[256,1152]{1,0:T(8,128)(2,1)S(1)}, u32[]{:S(2)}, u32[]{:S(2)}) %collective-permute-start.13) | collective-permute-done | bytes 589856 | tf_op jit(solution)/shard_map/ppermute | solution.py:101
  334.6 2.9 reshape.382
  340.1 3.6 collective-permute-done.11
  350.8 6.2 convolution_convert_fusion.2
  357.1 15.0 %multiply_convert_fusion = (bf16[1024,1728]{0,1:T(8,128)(2,1)}, bf16[1024,1728]{0,1:T(8,128)(2,1)}) fusion(f32[1024,1728]{0,1:T(8,128)} %fusion.120, f32[1024,1728]{0,1:T(8,128)} %get-tuple-element.117, bf16[1024,1152]{1,0:T(8,128)(2,1)S(1)} %bitcast.337, bf16[1152,1728]{1,0:T(8,128)(2,1)S(1)} %bitcast.323), kind=kOutput, calls=%fused_computation.13 | convolution fusion | flops 4119330816 | bytes 27574272 | tf_op jit(solution)/shard_map/rd,df->rf/dot_general | solution.py:47
  372.1 9.9 %convolution_convert_fusion = bf16[1152,1728]{0,1:T(8,128)(2,1)} fusion(bf16[1024,1728]{0,1:T(8,128)(2,1)} %get-tuple-element.39, bf16[1024,1152]{1,0:T(8,128)(2,1)S(1)} %bitcast.329), kind=kOutput, calls=%fused_computation.3 | convolution fusion | flops 4078854144 | bytes 9879552 | tf_op jit(solution)/shard_map/rd,rf->df/dot_general | solution.py:47
  382.0 5.0 fusion.121
  387.0 5.3 add_convert_fusion
  394.4 6.2 convolution_convert_fusion.1
  400.7 6.6 copy.199
  407.3 3.2 dynamic-slice_bitcast_fusion
  415.8 12.0 %collective-permute-done.16 = bf16[256,1152]{1,0:T(8,128)(2,1)S(1)} collective-permute-done((bf16[256,1152]{1,0:T(8,128)(2,1)S(1)}, bf16[256,1152]{1,0:T(8,128)(2,1)S(1)}, u32[]{:S(2)}, u32[]{:S(2)}) %collective-permute-start.16) | collective-permute-done | bytes 589856 | tf_op jit(solution)/shard_map/ppermute | solution.py:101
  437.3 6.5 copy.198
  443.7 13.9 %collective-permute-done.38 = bf16[4,144,1728]{2,1,0:T(8,128)(2,1)} collective-permute-done((bf16[4,144,1728]{2,1,0:T(8,128)(2,1)}, bf16[4,144,1728]{2,1,0:T(8,128)(2,1)}, u32[]{:S(2)}, u32[]{:S(2)}) %collective-permute-start.38) | collective-permute-done | bytes 1990688 | tf_op jit(solution)/shard_map/ppermute | solution.py:55
  470.2 6.4 copy.197
  476.7 3.1 dynamic-slice_bitcast_fusion.2
  481.3 21.1 %collective-permute-done.40 = bf16[144,1728]{1,0:T(8,128)(2,1)} collective-permute-done((bf16[144,1728]{1,0:T(8,128)(2,1)}, bf16[144,1728]{1,0:T(8,128)(2,1)}, u32[]{:S(2)}, u32[]{:S(2)}) %collective-permute-start.40) | collective-permute-done | bytes 497696 | tf_op jit(solution)/shard_map/ppermute | solution.py:80
  518.5 3.7 convolution_convert_fusion.6
  529.9 3.5 convolution_convert_fusion.7
  539.6 11.6 %collective-permute-start.35 = (bf16[144,1728]{1,0:T(8,128)(2,1)}, bf16[144,1728]{1,0:T(8,128)(2,1)}, u32[]{:S(2)}, u32[]{:S(2)}) collective-permute-start(bf16[144,1728]{1,0:T(8,128)(2,1)} %get-tuple-element.65), channel_id=1, source_target_pairs={{0,8},{8,16},{16,24},{24,0},{1,9},{9,17},{17,25},{25,1},{2,10},{10... | collective-permute-start | bytes 1493000 | tf_op jit(solution)/shard_map/ppermute | solution.py:80
  553.6 8.1 %collective-permute-done.30 = bf16[4,144,1728]{2,1,0:T(8,128)(2,1)} collective-permute-done((bf16[4,144,1728]{2,1,0:T(8,128)(2,1)}, bf16[4,144,1728]{2,1,0:T(8,128)(2,1)}, u32[]{:S(2)}, u32[]{:S(2)}) %collective-permute-start.30) | collective-permute-done | bytes 1990688 | tf_op jit(solution)/shard_map/ppermute | solution.py:55
  565.9 17.1 %collective-permute-done.19 = bf16[2,512,512]{1,2,0:T(8,128)(2,1)} collective-permute-done((bf16[2,512,512]{1,2,0:T(8,128)(2,1)}, bf16[2,512,512]{1,2,0:T(8,128)(2,1)}, u32[]{:S(2)}, u32[]{:S(2)}) %collective-permute-start.19) | collective-permute-done | bytes 1048608 | tf_op jit(solution)/shard_map/ppermute | solution.py:55
  595.3 2.7 fusion.18
  598.0 2.9 reshape.344
  603.5 2.9 reshape_reshape.25
  618.7 5.6 collective-permute-done.25
  628.7 7.3 %collective-permute-done.21 = bf16[256,1152]{1,0:T(8,128)(2,1)S(1)} collective-permute-done((bf16[256,1152]{1,0:T(8,128)(2,1)}, bf16[256,1152]{1,0:T(8,128)(2,1)S(1)}, u32[]{:S(2)}, u32[]{:S(2)}) %collective-permute-start.21) | collective-permute-done | bytes 589856 | tf_op jit(solution)/shard_map/ppermute | solution.py:101
  641.4 4.9 collective-permute-done.26
  647.8 10.2 %collective-permute-start.27 = (bf16[192,512]{1,0:T(8,128)(2,1)S(1)}, bf16[192,512]{1,0:T(8,128)(2,1)S(1)}, u32[]{:S(2)}, u32[]{:S(2)}) collective-permute-start(bf16[192,512]{1,0:T(8,128)(2,1)S(1)} %get-tuple-element.91), channel_id=1, source_target_pairs={{0,8},{8,16},{16,24},{24,0},{1,9},{9,17},{17,25},{25,1},{2,10},{10... | collective-permute-start | bytes 589832 | tf_op jit(solution)/shard_map/ppermute | solution.py:80
  662.0 45.2 %all-gather.4 = f32[1024,160]{1,0:T(8,128)S(1)} all-gather(f32[32,160]{1,0:T(8,128)S(1)} %concatenate.69), channel_id=6, replica_groups=mesh['dp'=4,'seq'=2,'tensor'=4] {'dp','seq','tensor'}, dimensions={0}, use_global_device_ids=true | all-gather | bytes 675840 | tf_op jit(solution)/shard_map/all_gather | solution.py:307
  (423 shorter events, 186.6 us)
Async XLA Ops:
  7.2 63.8 %all-gather.10.cloned.1.call-start = ((), (), s32[]{:S(2)}) async-start(), calls=%async_computation | async-start | bytes 1622016 | tf_op jit(solution)/shard_map/all_gather | solution.py:173
  12.9 115.9 %all-gather.12.cloned.1.call-start = ((), (), s32[]{:S(2)}) async-start(), calls=%async_computation.1 | async-start | bytes 2580480 | tf_op jit(solution)/shard_map/all_gather | solution.py:69
  13.7 148.7 %all-gather.14.cloned.1.call-start = ((), (), s32[]{:S(2)}) async-start(), calls=%async_computation.2 | async-start | bytes 2580480 | tf_op jit(solution)/shard_map/all_gather | solution.py:69
  33.5 13.6 %collective-permute-start = (bf16[4,144,512]{2,1,0:T(8,128)(2,1)S(1)}, bf16[4,144,512]{2,1,0:T(8,128)(2,1)S(1)}, u32[]{:S(2)}, u32[]{:S(2)}) collective-permute-start(bf16[4,144,512]{2,1,0:T(8,128)(2,1)S(1)} %bitcast.324), channel_id=1, source_target_pairs={{0,4},{4,0},{1,5},{5,1},{2,6},{6,2},{3,7},{7,3},{8,12},{12,8},{9,1... | collective-permute-start | bytes 1769480 | tf_op jit(solution)/shard_map/ppermute | solution.py:55
  35.1 172.7 %all-gather.16.cloned.1.call-start = ((), (), s32[]{:S(2)}) async-start(), calls=%async_computation.3 | async-start | bytes 2580480 | tf_op jit(solution)/shard_map/all_gather | solution.py:69
  35.2 46.8 %copy-start.68 = (f32[2,512]{1,0:T(2,128)}, f32[2,512]{1,0:T(2,128)S(1)}, u32[]{:S(2)}) copy-start(f32[2,512]{1,0:T(2,128)S(1)} %convert_element_type.331) | copy-start | bytes 12292
  35.2 46.8 %copy-start.88 = (f32[128]{0:T(128)}, f32[128]{0:T(128)S(1)}, u32[]{:S(2)}) copy-start(f32[128]{0:T(128)S(1)} %negate_power_fusion) | copy-start | bytes 1540
  85.5 25.6 %collective-permute-start.1 = (bf16[2,512,512]{1,2,0:T(8,128)(2,1)}, bf16[2,512,512]{1,2,0:T(8,128)(2,1)}, u32[]{:S(2)}, u32[]{:S(2)}) collective-permute-start(bf16[2,512,512]{1,2,0:T(8,128)(2,1)} %pad_maximum_fusion.15), channel_id=1, source_target_pairs={{0,4},{4,0},{1,5},{5,1},{2,6},{6,2},{3,7},{7,3},{8,12},{12,8},{9,1... | collective-permute-start | bytes 3145736 | tf_op jit(solution)/shard_map/ppermute | solution.py:55
  122.6 3.0 collective-permute-start.2
  127.3 83.7 %collective-permute-start.3 = (bf16[256,1152]{1,0:T(8,128)(2,1)S(1)}, bf16[256,1152]{1,0:T(8,128)(2,1)S(1)}, u32[]{:S(2)}, u32[]{:S(2)}) collective-permute-start(bf16[256,1152]{1,0:T(8,128)(2,1)S(1)} %dynamic-slice_bitcast_fusion.12), channel_id=1, source_target_pairs={{0,2},{1,3},{2,0},{3,1},{4,6},{5,7},{6,4},{7,5},{8,10},{9,11},{10,... | collective-permute-start | bytes 1769480 | tf_op jit(solution)/shard_map/ppermute | solution.py:101
  128.8 86.5 %collective-permute-start.6 = (bf16[4,144,1728]{2,1,0:T(8,128)(2,1)}, bf16[4,144,1728]{2,1,0:T(8,128)(2,1)}, u32[]{:S(2)}, u32[]{:S(2)}) collective-permute-start(bf16[4,144,1728]{2,1,0:T(8,128)(2,1)} %bitcast.339), channel_id=1, source_target_pairs={{0,4},{4,0},{1,5},{5,1},{2,6},{6,2},{3,7},{7,3},{8,12},{12,8},{9,1... | collective-permute-start | bytes 5971976 | tf_op jit(solution)/shard_map/ppermute | solution.py:55
  162.3 58.9 %collective-permute-start.7 = (bf16[4,144,1728]{2,1,0:T(8,128)(2,1)}, bf16[4,144,1728]{2,1,0:T(8,128)(2,1)}, u32[]{:S(2)}, u32[]{:S(2)}) collective-permute-start(bf16[4,144,1728]{2,1,0:T(8,128)(2,1)} %bitcast.341), channel_id=1, source_target_pairs={{0,4},{4,0},{1,5},{5,1},{2,6},{6,2},{3,7},{7,3},{8,12},{12,8},{9,1... | collective-permute-start | bytes 5971976 | tf_op jit(solution)/shard_map/ppermute | solution.py:55
  207.8 56.5 %collective-permute-start.8 = (bf16[4,144,1728]{2,1,0:T(8,128)(2,1)}, bf16[4,144,1728]{2,1,0:T(8,128)(2,1)}, u32[]{:S(2)}, u32[]{:S(2)}) collective-permute-start(bf16[4,144,1728]{2,1,0:T(8,128)(2,1)} %bitcast.343), channel_id=1, source_target_pairs={{0,4},{4,0},{1,5},{5,1},{2,6},{6,2},{3,7},{7,3},{8,12},{12,8},{9,1... | collective-permute-start | bytes 5971976 | tf_op jit(solution)/shard_map/ppermute | solution.py:55
  213.8 14.9 %collective-permute-start.4 = (bf16[256,1152]{1,0:T(8,128)(2,1)S(1)}, bf16[256,1152]{1,0:T(8,128)(2,1)S(1)}, u32[]{:S(2)}, u32[]{:S(2)}) collective-permute-start(bf16[256,1152]{1,0:T(8,128)(2,1)S(1)} %multiply_convert_fusion.4), channel_id=1, source_target_pairs={{0,2},{1,3},{2,0},{3,1},{4,6},{5,7},{6,4},{7,5},{8,10},{9,11},{10,... | collective-permute-start | bytes 1769480 | tf_op jit(solution)/shard_map/ppermute | solution.py:101
  229.1 37.5 %collective-permute-start.5 = (bf16[2,256,1152]{2,1,0:T(8,128)(2,1)S(1)}, bf16[2,256,1152]{2,1,0:T(8,128)(2,1)S(1)}, u32[]{:S(2)}, u32[]{:S(2)}) collective-permute-start(bf16[2,256,1152]{2,1,0:T(8,128)(2,1)S(1)} %pad_maximum_fusion.10), channel_id=1, source_target_pairs={{0,1},{1,0},{2,3},{3,2},{4,5},{5,4},{6,7},{7,6},{8,9},{9,8},{10,11... | collective-permute-start | bytes 3538952 | tf_op jit(solution)/shard_map/ppermute | solution.py:101
  290.3 2.9 collective-permute-start.9
  294.4 15.7 %collective-permute-start.10 = (bf16[256,1152]{1,0:T(8,128)(2,1)}, bf16[256,1152]{1,0:T(8,128)(2,1)}, u32[]{:S(2)}, u32[]{:S(2)}) collective-permute-start(bf16[256,1152]{1,0:T(8,128)(2,1)} %dynamic-slice_bitcast_fusion.11), channel_id=1, source_target_pairs={{0,2},{1,3},{2,0},{3,1},{4,6},{5,7},{6,4},{7,5},{8,10},{9,11},{10,... | collective-permute-start | bytes 1769480 | tf_op jit(solution)/shard_map/ppermute | solution.py:101
  316.4 16.3 %collective-permute-start.13 = (bf16[256,1152]{1,0:T(8,128)(2,1)S(1)}, bf16[256,1152]{1,0:T(8,128)(2,1)S(1)}, u32[]{:S(2)}, u32[]{:S(2)}) collective-permute-start(bf16[256,1152]{1,0:T(8,128)(2,1)S(1)} %get-tuple-element.71), channel_id=1, source_target_pairs={{0,2},{1,3},{2,0},{3,1},{4,6},{5,7},{6,4},{7,5},{8,10},{9,11},{10,... | collective-permute-start | bytes 1769480 | tf_op jit(solution)/shard_map/ppermute | solution.py:101
  317.0 26.7 %collective-permute-start.11 = (bf16[256,1152]{1,0:T(8,128)(2,1)}, bf16[256,1152]{1,0:T(8,128)(2,1)}, u32[]{:S(2)}, u32[]{:S(2)}) collective-permute-start(bf16[256,1152]{1,0:T(8,128)(2,1)} %get-tuple-element.72), channel_id=1, source_target_pairs={{0,2},{1,3},{2,0},{3,1},{4,6},{5,7},{6,4},{7,5},{8,10},{9,11},{10,... | collective-permute-start | bytes 1769480 | tf_op jit(solution)/shard_map/ppermute | solution.py:101
  334.0 13.0 %collective-permute-start.14 = (bf16[2,256,1152]{2,1,0:T(8,128)(2,1)}, bf16[2,256,1152]{2,1,0:T(8,128)(2,1)}, u32[]{:S(2)}, u32[]{:S(2)}) collective-permute-start(bf16[2,256,1152]{2,1,0:T(8,128)(2,1)} %pad_maximum_fusion.12), channel_id=1, source_target_pairs={{0,1},{1,0},{2,3},{3,2},{4,5},{5,4},{6,7},{7,6},{8,9},{9,8},{10,11... | collective-permute-start | bytes 3538952 | tf_op jit(solution)/shard_map/ppermute | solution.py:101
  347.0 67.1 %collective-permute-start.12 = (bf16[2,256,1152]{2,1,0:T(8,128)(2,1)}, bf16[2,256,1152]{2,1,0:T(8,128)(2,1)}, u32[]{:S(2)}, u32[]{:S(2)}) collective-permute-start(bf16[2,256,1152]{2,1,0:T(8,128)(2,1)} %pad_maximum_fusion.11), channel_id=1, source_target_pairs={{0,1},{1,0},{2,3},{3,2},{4,5},{5,4},{6,7},{7,6},{8,9},{9,8},{10,11... | collective-permute-start | bytes 3538952 | tf_op jit(solution)/shard_map/ppermute | solution.py:101
  393.9 17.1 %collective-permute-start.15 = (bf16[2,256,1152]{2,1,0:T(8,128)(2,1)S(1)}, bf16[2,256,1152]{2,1,0:T(8,128)(2,1)}, u32[]{:S(2)}, u32[]{:S(2)}) collective-permute-start(bf16[2,256,1152]{2,1,0:T(8,128)(2,1)S(1)} %dynamic-slice_bitcast_fusion.4), channel_id=1, source_target_pairs={{0,1},{1,0},{2,3},{3,2},{4,5},{5,4},{6,7},{7,6},{8,9},{9,8},{10,11... | collective-permute-start | bytes 3538952 | tf_op jit(solution)/shard_map/ppermute | solution.py:101
  410.4 47.2 %collective-permute-start.38 = (bf16[4,144,1728]{2,1,0:T(8,128)(2,1)}, bf16[4,144,1728]{2,1,0:T(8,128)(2,1)}, u32[]{:S(2)}, u32[]{:S(2)}) collective-permute-start(bf16[4,144,1728]{2,1,0:T(8,128)(2,1)} %dynamic-slice_bitcast_fusion), channel_id=1, source_target_pairs={{0,4},{4,0},{1,5},{5,1},{2,6},{6,2},{3,7},{7,3},{8,12},{12,8},{9,1... | collective-permute-start | bytes 5971976 | tf_op jit(solution)/shard_map/ppermute | solution.py:55
  412.6 15.2 %collective-permute-start.16 = (bf16[256,1152]{1,0:T(8,128)(2,1)S(1)}, bf16[256,1152]{1,0:T(8,128)(2,1)S(1)}, u32[]{:S(2)}, u32[]{:S(2)}) collective-permute-start(bf16[256,1152]{1,0:T(8,128)(2,1)S(1)} %dynamic-slice_bitcast_fusion.10), channel_id=1, source_target_pairs={{0,2},{1,3},{2,0},{3,1},{4,6},{5,7},{6,4},{7,5},{8,10},{9,11},{10,... | collective-permute-start | bytes 1769480 | tf_op jit(solution)/shard_map/ppermute | solution.py:101
  432.5 27.8 %collective-permute-start.17 = (bf16[256,1152]{1,0:T(8,128)(2,1)}, bf16[256,1152]{1,0:T(8,128)(2,1)}, u32[]{:S(2)}, u32[]{:S(2)}) collective-permute-start(bf16[256,1152]{1,0:T(8,128)(2,1)} %multiply_convert_fusion.3), channel_id=1, source_target_pairs={{0,2},{1,3},{2,0},{3,1},{4,6},{5,7},{6,4},{7,5},{8,10},{9,11},{10,... | collective-permute-start | bytes 1769480 | tf_op jit(solution)/shard_map/ppermute | solution.py:101
  462.8 42.1 %collective-permute-start.18 = (bf16[2,256,1152]{2,1,0:T(8,128)(2,1)}, bf16[2,256,1152]{2,1,0:T(8,128)(2,1)}, u32[]{:S(2)}, u32[]{:S(2)}) collective-permute-start(bf16[2,256,1152]{2,1,0:T(8,128)(2,1)} %pad_maximum_fusion.13), channel_id=1, source_target_pairs={{0,1},{1,0},{2,3},{3,2},{4,5},{5,4},{6,7},{7,6},{8,9},{9,8},{10,11... | collective-permute-start | bytes 3538952 | tf_op jit(solution)/shard_map/ppermute | solution.py:101
  464.0 16.8 %collective-permute-start.39 = (bf16[144,1728]{1,0:T(8,128)(2,1)}, bf16[144,1728]{1,0:T(8,128)(2,1)}, u32[]{:S(2)}, u32[]{:S(2)}) collective-permute-start(bf16[144,1728]{1,0:T(8,128)(2,1)} %get-tuple-element.62), channel_id=1, source_target_pairs={{0,8},{8,16},{16,24},{24,0},{1,9},{9,17},{17,25},{25,1},{2,10},{10... | collective-permute-start | bytes 1493000 | tf_op jit(solution)/shard_map/ppermute | solution.py:80
  464.5 37.9 %collective-permute-start.40 = (bf16[144,1728]{1,0:T(8,128)(2,1)}, bf16[144,1728]{1,0:T(8,128)(2,1)}, u32[]{:S(2)}, u32[]{:S(2)}) collective-permute-start(bf16[144,1728]{1,0:T(8,128)(2,1)} %get-tuple-element.64), channel_id=1, source_target_pairs={{0,16},{8,24},{16,0},{24,8},{1,17},{9,25},{17,1},{25,9},{2,18},{10... | collective-permute-start | bytes 1493000 | tf_op jit(solution)/shard_map/ppermute | solution.py:80
  466.8 35.7 %collective-permute-start.41 = (bf16[144,1728]{1,0:T(8,128)(2,1)}, bf16[144,1728]{1,0:T(8,128)(2,1)}, u32[]{:S(2)}, u32[]{:S(2)}) collective-permute-start(bf16[144,1728]{1,0:T(8,128)(2,1)} %get-tuple-element.63), channel_id=1, source_target_pairs={{0,24},{8,0},{16,8},{24,16},{1,25},{9,1},{17,9},{25,17},{2,26},{10... | collective-permute-start | bytes 1493000 | tf_op jit(solution)/shard_map/ppermute | solution.py:80
  469.3 66.6 %collective-permute-start.34 = (bf16[4,144,1728]{2,1,0:T(8,128)(2,1)}, bf16[4,144,1728]{2,1,0:T(8,128)(2,1)}, u32[]{:S(2)}, u32[]{:S(2)}) collective-permute-start(bf16[4,144,1728]{2,1,0:T(8,128)(2,1)} %dynamic-slice_bitcast_fusion.1), channel_id=1, source_target_pairs={{0,4},{4,0},{1,5},{5,1},{2,6},{6,2},{3,7},{7,3},{8,12},{12,8},{9,1... | collective-permute-start | bytes 5971976 | tf_op jit(solution)/shard_map/ppermute | solution.py:55
  480.8 80.8 %collective-permute-start.30 = (bf16[4,144,1728]{2,1,0:T(8,128)(2,1)}, bf16[4,144,1728]{2,1,0:T(8,128)(2,1)}, u32[]{:S(2)}, u32[]{:S(2)}) collective-permute-start(bf16[4,144,1728]{2,1,0:T(8,128)(2,1)} %dynamic-slice_bitcast_fusion.2), channel_id=1, source_target_pairs={{0,4},{4,0},{1,5},{5,1},{2,6},{6,2},{3,7},{7,3},{8,12},{12,8},{9,1... | collective-permute-start | bytes 5971976 | tf_op jit(solution)/shard_map/ppermute | solution.py:55
  526.8 56.3 %collective-permute-start.19 = (bf16[2,512,512]{1,2,0:T(8,128)(2,1)}, bf16[2,512,512]{1,2,0:T(8,128)(2,1)}, u32[]{:S(2)}, u32[]{:S(2)}) collective-permute-start(bf16[2,512,512]{1,2,0:T(8,128)(2,1)} %fusion.50), channel_id=1, source_target_pairs={{0,4},{4,0},{1,5},{5,1},{2,6},{6,2},{3,7},{7,3},{8,12},{12,8},{9,1... | collective-permute-start | bytes 3145736 | tf_op jit(solution)/shard_map/ppermute | solution.py:55
  539.6 68.0 %collective-permute-start.35 = (bf16[144,1728]{1,0:T(8,128)(2,1)}, bf16[144,1728]{1,0:T(8,128)(2,1)}, u32[]{:S(2)}, u32[]{:S(2)}) collective-permute-start(bf16[144,1728]{1,0:T(8,128)(2,1)} %get-tuple-element.65), channel_id=1, source_target_pairs={{0,8},{8,16},{16,24},{24,0},{1,9},{9,17},{17,25},{25,1},{2,10},{10... | collective-permute-start | bytes 1493000 | tf_op jit(solution)/shard_map/ppermute | solution.py:80
  551.2 57.8 %collective-permute-start.36 = (bf16[144,1728]{1,0:T(8,128)(2,1)}, bf16[144,1728]{1,0:T(8,128)(2,1)}, u32[]{:S(2)}, u32[]{:S(2)}) collective-permute-start(bf16[144,1728]{1,0:T(8,128)(2,1)} %get-tuple-element.67), channel_id=1, source_target_pairs={{0,16},{8,24},{16,0},{24,8},{1,17},{9,25},{17,1},{25,9},{2,18},{10... | collective-permute-start | bytes 1493000 | tf_op jit(solution)/shard_map/ppermute | solution.py:80
  551.6 57.4 %collective-permute-start.37 = (bf16[144,1728]{1,0:T(8,128)(2,1)}, bf16[144,1728]{1,0:T(8,128)(2,1)}, u32[]{:S(2)}, u32[]{:S(2)}) collective-permute-start(bf16[144,1728]{1,0:T(8,128)(2,1)} %get-tuple-element.66), channel_id=1, source_target_pairs={{0,24},{8,0},{16,8},{24,16},{1,25},{9,1},{17,9},{25,17},{2,26},{10... | collective-permute-start | bytes 1493000 | tf_op jit(solution)/shard_map/ppermute | solution.py:80
  565.0 73.6 %collective-permute-start.31 = (bf16[144,1728]{1,0:T(8,128)(2,1)}, bf16[144,1728]{1,0:T(8,128)(2,1)}, u32[]{:S(2)}, u32[]{:S(2)}) collective-permute-start(bf16[144,1728]{1,0:T(8,128)(2,1)} %get-tuple-element.68), channel_id=1, source_target_pairs={{0,8},{8,16},{16,24},{24,0},{1,9},{9,17},{17,25},{25,1},{2,10},{10... | collective-permute-start | bytes 1493000 | tf_op jit(solution)/shard_map/ppermute | solution.py:80
  583.1 55.4 %collective-permute-start.32 = (bf16[144,1728]{1,0:T(8,128)(2,1)}, bf16[144,1728]{1,0:T(8,128)(2,1)}, u32[]{:S(2)}, u32[]{:S(2)}) collective-permute-start(bf16[144,1728]{1,0:T(8,128)(2,1)} %get-tuple-element.70), channel_id=1, source_target_pairs={{0,16},{8,24},{16,0},{24,8},{1,17},{9,25},{17,1},{25,9},{2,18},{10... | collective-permute-start | bytes 1493000 | tf_op jit(solution)/shard_map/ppermute | solution.py:80
  607.7 30.9 %collective-permute-start.33 = (bf16[144,1728]{1,0:T(8,128)(2,1)}, bf16[144,1728]{1,0:T(8,128)(2,1)}, u32[]{:S(2)}, u32[]{:S(2)}) collective-permute-start(bf16[144,1728]{1,0:T(8,128)(2,1)} %get-tuple-element.69), channel_id=1, source_target_pairs={{0,24},{8,0},{16,8},{24,16},{1,25},{9,1},{17,9},{25,17},{2,26},{10... | collective-permute-start | bytes 1493000 | tf_op jit(solution)/shard_map/ppermute | solution.py:80
  609.0 6.0 collective-permute-start.20
  609.0 5.1 collective-permute-start.24
  614.4 9.9 %collective-permute-start.25 = (bf16[288,512]{1,0:T(8,128)(2,1)S(1)}, bf16[288,512]{1,0:T(8,128)(2,1)S(1)}, u32[]{:S(2)}, u32[]{:S(2)}) collective-permute-start(bf16[288,512]{1,0:T(8,128)(2,1)S(1)} %dynamic-slice_bitcast_fusion.22), channel_id=1, source_target_pairs={{0,2},{1,3},{2,0},{3,1},{4,6},{5,7},{6,4},{7,5},{8,10},{9,11},{10,... | collective-permute-start | bytes 884744 | tf_op jit(solution)/shard_map/ppermute | solution.py:101
  617.2 18.8 %collective-permute-start.21 = (bf16[256,1152]{1,0:T(8,128)(2,1)}, bf16[256,1152]{1,0:T(8,128)(2,1)S(1)}, u32[]{:S(2)}, u32[]{:S(2)}) collective-permute-start(bf16[256,1152]{1,0:T(8,128)(2,1)} %dynamic-slice_bitcast_fusion.9), channel_id=1, source_target_pairs={{0,2},{1,3},{2,0},{3,1},{4,6},{5,7},{6,4},{7,5},{8,10},{9,11},{10,... | collective-permute-start | bytes 1769480 | tf_op jit(solution)/shard_map/ppermute | solution.py:101
  628.1 18.2 %collective-permute-start.26 = (bf16[4,192,512]{2,1,0:T(8,128)(2,1)}, bf16[4,192,512]{2,1,0:T(8,128)(2,1)}, u32[]{:S(2)}, u32[]{:S(2)}) collective-permute-start(bf16[4,192,512]{2,1,0:T(8,128)(2,1)} %dynamic-slice_bitcast_fusion.7), channel_id=1, source_target_pairs={{0,4},{4,0},{1,5},{5,1},{2,6},{6,2},{3,7},{7,3},{8,12},{12,8},{9,1... | collective-permute-start | bytes 2359304 | tf_op jit(solution)/shard_map/ppermute | solution.py:55
  637.9 22.7 %collective-permute-start.22 = (bf16[256,1152]{1,0:T(8,128)(2,1)}, bf16[256,1152]{1,0:T(8,128)(2,1)S(1)}, u32[]{:S(2)}, u32[]{:S(2)}) collective-permute-start(bf16[256,1152]{1,0:T(8,128)(2,1)} %fusion.39), channel_id=1, source_target_pairs={{0,2},{1,3},{2,0},{3,1},{4,6},{5,7},{6,4},{7,5},{8,10},{9,11},{10,... | collective-permute-start | bytes 1769480 | tf_op jit(solution)/shard_map/ppermute | solution.py:101
  647.8 60.7 %collective-permute-start.27 = (bf16[192,512]{1,0:T(8,128)(2,1)S(1)}, bf16[192,512]{1,0:T(8,128)(2,1)S(1)}, u32[]{:S(2)}, u32[]{:S(2)}) collective-permute-start(bf16[192,512]{1,0:T(8,128)(2,1)S(1)} %get-tuple-element.91), channel_id=1, source_target_pairs={{0,8},{8,16},{16,24},{24,0},{1,9},{9,17},{17,25},{25,1},{2,10},{10... | collective-permute-start | bytes 589832 | tf_op jit(solution)/shard_map/ppermute | solution.py:80
  657.9 50.5 %collective-permute-start.28 = (bf16[192,512]{1,0:T(8,128)(2,1)S(1)}, bf16[192,512]{1,0:T(8,128)(2,1)S(1)}, u32[]{:S(2)}, u32[]{:S(2)}) collective-permute-start(bf16[192,512]{1,0:T(8,128)(2,1)S(1)} %get-tuple-element.93), channel_id=1, source_target_pairs={{0,16},{8,24},{16,0},{24,8},{1,17},{9,25},{17,1},{25,9},{2,18},{10... | collective-permute-start | bytes 589832 | tf_op jit(solution)/shard_map/ppermute | solution.py:80
  657.9 50.5 %collective-permute-start.29 = (bf16[192,512]{1,0:T(8,128)(2,1)S(1)}, bf16[192,512]{1,0:T(8,128)(2,1)S(1)}, u32[]{:S(2)}, u32[]{:S(2)}) collective-permute-start(bf16[192,512]{1,0:T(8,128)(2,1)S(1)} %get-tuple-element.92), channel_id=1, source_target_pairs={{0,24},{8,0},{16,8},{24,16},{1,25},{9,1},{17,9},{25,17},{2,26},{10... | collective-permute-start | bytes 589832 | tf_op jit(solution)/shard_map/ppermute | solution.py:80
  661.9 48.0 %collective-permute-start.23 = (bf16[2,256,1152]{2,1,0:T(8,128)(2,1)S(1)}, bf16[2,256,1152]{2,1,0:T(8,128)(2,1)S(1)}, u32[]{:S(2)}, u32[]{:S(2)}) collective-permute-start(bf16[2,256,1152]{2,1,0:T(8,128)(2,1)S(1)} %pad_maximum_fusion.14), channel_id=1, source_target_pairs={{0,1},{1,0},{2,3},{3,2},{4,5},{5,4},{6,7},{7,6},{8,9},{9,8},{10,11... | collective-permute-start | bytes 3538952 | tf_op jit(solution)/shard_map/ppermute | solution.py:101
  (93 other events, 859.7 us)
Sparse Core Ops, SparseCore 0:
  13.1 57.8 all-gather.9
  72.5 44.1 all-gather.11
  118.3 43.9 all-gather.13
  163.8 43.9 all-gather.15

commit v3 on v2

--- a/solution.py
+++ b/solution.py
@@ -130,6 +130,38 @@
     other = across(both, 1)
     full = jnp.stack([jnp.where(even, both, other), jnp.where(even, other, both)], axis=1)
     return full.reshape(-1, share.shape[-1])
+
+
+def gather_pack(shard):
+    seq_n, dp_n = lax.axis_size("seq"), lax.axis_size("dp")
+    if seq_n != 2:
+        return lax.all_gather(shard, ("dp", "seq"), axis=0, tiled=False)
+    me = lax.axis_index("dp")
+    came = [shard]
+    for step in range(1, dp_n):
+        came.append(
+            lax.ppermute(shard, "dp", [(index, (index + step) % dp_n) for index in range(dp_n)])
+        )
+    both = jnp.stack([in_order(entry, swap(entry), 0) for entry in came], axis=0)
+    ordered = [
+        lax.dynamic_index_in_dim(both, lax.rem(me - index + dp_n, dp_n), 0, keepdims=False)
+        for index in range(dp_n)
+    ]
+    return jnp.concatenate(ordered, axis=0)
+
+
+def add_gains(terms):
+    seq_n, tensor_n = lax.axis_size("seq"), lax.axis_size("tensor")
+    if seq_n != 2 or tensor_n != 4:
+        return lax.psum_scatter(terms, ALL, scatter_dimension=0, tiled=True)[0]
+    dp_n = lax.axis_size("dp")
+    parts = terms.reshape(dp_n, 2, 4, -1)
+    for bit in (1, 2):
+        parts = parts + across(parts, bit)
+    parts = lax.dynamic_index_in_dim(parts, lax.axis_index("tensor"), 2, keepdims=False)
+    parts = parts + swap(parts)
+    parts = lax.dynamic_index_in_dim(parts, lax.axis_index("seq"), 1, keepdims=False)
+    return add_dp(parts)
 
 
 def row_sum(values):
@@ -170,9 +202,12 @@
     gain_n = gain_row.shape[0]
     gain_row = jnp.pad(gain_row, (0, 2 * head - gain_n))[None]
     fill = jnp.zeros((-(part + 1) % 16, 2 * head), LOW)
-    small = lax.all_gather(
-        jnp.concatenate([kv_weight, gain_row, fill], axis=0), ALL, axis=0, tiled=True
-    ).reshape(all_n, -1, 2 * head)
+    small = spread(jnp.concatenate([kv_weight, gain_row, fill], axis=0))
+    qo_weight = jnp.concatenate([q_weight, o_weight.T], axis=1)
+    own_n = width // blocks_n
+    pack = gather_pack(jnp.concatenate([qo_weight, small], axis=0))
+    qo_mat = pack[:, :own_n].reshape(width, 2 * head)
+    small = pack[:, own_n:].reshape(all_n, -1, 2 * head)
     kv_mat = small[:, :part].reshape(width, 2 * head)
     gains = small[:, part, :gain_n].astype(F32)
 
@@ -184,7 +219,6 @@
     scale_q = 1.0 + gains[:, tail : tail + head_part].reshape(head)
     scale_k = 1.0 + gains[:, tail + head_part :].reshape(head)
 
-    qo_mat = gather_rows(jnp.concatenate([q_weight, o_weight.T], axis=1))
     q_mat, o_mat = qo_mat[:, :head], qo_mat[:, head:]
     gate_mat = gather_rows(gate_weight)
     up_mat = gather_rows(up_weight)
@@ -237,7 +271,7 @@
     ffn_hat, ffn_fac = normalize(ffn_out)
     g_fo = row_sum(back * ffn_hat)
     d_ffn = spread(norm_back(ffn_hat, ffn_fac, back * scale_fo).astype(LOW))
-    result = spread((middle + ffn_hat * scale_fo).astype(LOW)).reshape(tokens.shape)
+    result = (middle + ffn_hat * scale_fo).astype(LOW)
 
     g_down = product("rd,rf->df", d_ffn, acted).astype(LOW)
     d_ffn, g_down = lax.optimization_barrier((d_ffn, g_down))
@@ -262,6 +296,8 @@
 
     g_out = product("rd,re->de", d_branch, attended_r)
     d_att = product("rd,de->re", d_branch, o_mat).astype(LOW).reshape(attended.shape)
+    d_att, result = lax.optimization_barrier((d_att, result))
+    result = spread(result).reshape(tokens.shape)
     d_probs = product("sqd,skd->sqk", d_att, value_all)
     row_dot = jnp.sum(probs * d_probs, axis=-1, keepdims=True)
     d_scores = (probs * (d_probs - row_dot)).astype(LOW)
@@ -297,16 +333,13 @@
     fill = jnp.zeros((blocks_n, -(width // blocks_n + part) % 16, 2 * head), LOW)
     last = jnp.concatenate([g_qo, g_kv, fill], axis=1).reshape(-1, 2 * head)
     last = scatter_rows(last)
-    own_n = width // blocks_n
     g_ai = row_sum(d_normed * in_hat)
     d_input = d_middle + norm_back(in_hat, in_fac, d_normed * scale_ai)
     d_input = spread(d_input.astype(LOW)).reshape(tokens.shape)
     gain_terms = jnp.concatenate(
         [entry.reshape(all_n, -1) for entry in (g_ai, g_ao, g_fi, g_fo, g_q, g_k)], axis=1
     )
-    gain_all = lax.all_gather(gain_terms, ALL, axis=0, tiled=False)
-    own = lax.dynamic_index_in_dim(gain_all, lax.axis_index(ALL), 1, keepdims=False)
-    gain_sums = jnp.sum(own, axis=0)
+    gain_sums = add_gains(gain_terms)
     return (
         result,
         d_input,

time: 731 us -> 749 us (1.025)
  waiting for transfers between devices: 307 us -> 390 us
  blocking collectives: 64.1 us -> 0 us
    ppermute x12 -> x15, waiting for transfers between devices: 22.2 us -> 104 us  [add_dp(): lax.ppermute(sent, 'dp', [(index, (index + step) % dp_n) for index in ran...]
    all_gather x2 -> x0, blocking collectives: 64.1 us -> none  [the longest x1 45.2 us: body(): gain_all = lax.all_gather(gain_terms, ALL, axis=0, tiled=False)]
    ppermute x0 -> x3, waiting for transfers between devices: none -> 55.5 us  [gather_pack(): lax.ppermute(shard, 'dp', [(index, (index + step) % dp_n) for index in ra...]
    all_gather x3, waiting for transfers between devices: 77 us -> 29.3 us  [gather_rows(): mine = lax.all_gather(shard, 'dp', axis=0, tiled=False)]
    all_gather x1 -> x0, waiting for transfers between devices: 23.5 us -> none  [body(): lax.all_gather(jnp.concatenate([kv_weight, gain_row, fill], axis=0), ALL,...]
    ppermute x10 -> x14, waiting for transfers between devices: 117 us -> 133 us  [swap(): return lax.ppermute(values, 'seq', [(0, 1), (1, 0)])]
    ppermute x12 -> x15, starting transfers between devices: 34.5 us -> 21.3 us  [add_dp(): lax.ppermute(sent, 'dp', [(index, (index + step) % dp_n) for index in ran...]
    ppermute x10 -> x14, starting transfers between devices: 9.5 us -> 19.7 us  [swap(): return lax.ppermute(values, 'seq', [(0, 1), (1, 0)])]
  transfers between devices with their start and end apart: 46 -> 59, of which waited for: 22 -> 31; matrix products, arithmetic and copies ran while one was open for 31% -> 24% of each run, Pallas kernels for 0% -> 0%
where the time goes in v3:
time: 749 us; the launch traced here: 741 us
  waiting for transfers between devices  390 us (52%)
  matrix products  103 us (14%)
  local copies, waits for them, and re-layouts  90.9 us (12%)
  other arithmetic  80.3 us (11%)
  starting transfers between devices  60.9 us (8%)
  between operations  16 us (2%)
    ppermute x14, waiting for transfers between devices, swap(): return lax.ppermute(values, 'seq', [(0, 1), (1, 0)])  133 us
    ppermute x15, waiting for transfers between devices, add_dp(): lax.ppermute(sent, 'dp', [(index, (index + step) % dp_n) for index in ran...  104 us
    dot_general x24, matrix products, product(): return jnp.einsum(pattern, left_m, right_m, preferred_element_type=F32)  103 us
    ppermute x24, waiting for transfers between devices, across(): lax.ppermute(values, 'tensor', [(index, index ^ bit) for index in range(4)])  68.4 us
    ppermute x3, waiting for transfers between devices, gather_pack(): lax.ppermute(shard, 'dp', [(index, (index + step) % dp_n) for index in ra...  55.5 us
    all_gather x3, waiting for transfers between devices, gather_rows(): mine = lax.all_gather(shard, 'dp', axis=0, tiled=False)  29.3 us
    ppermute x15, starting transfers between devices, add_dp(): lax.ppermute(sent, 'dp', [(index, (index + step) % dp_n) for index in ran...  21.3 us
    ppermute x14, starting transfers between devices, swap(): return lax.ppermute(values, 'seq', [(0, 1), (1, 0)])  19.7 us
  transfers between devices with their start and end apart: 59, of which 31 were waited for; matrix products, arithmetic and copies ran while one was open for 24% of the time, Pallas kernels for 0%

profile of v3, /device:TPU:0, one launch (start us, length us, event | category | flops | bytes accessed | tf_op | source)
XLA Modules:
  0.0 741.1 jit_solution(1211772946589878108)
XLA Ops:
  7.2 4.2 concatenate.74
  12.4 3.0 collective-permute-start
  28.8 26.0 %collective-permute-done.7 = bf16[336,512]{1,0:T(8,128)(2,1)} collective-permute-done((bf16[336,512]{1,0:T(8,128)(2,1)}, bf16[336,512]{1,0:T(8,128)(2,1)}, u32[]{:S(2)}, u32[]{:S(2)}) %collective-permute-start.7) | collective-permute-done | bytes 344096 | tf_op jit(solution)/shard_map/ppermute | solution.py:143
  56.9 29.6 %collective-permute-done.5 = bf16[336,512]{1,0:T(8,128)(2,1)S(1)} collective-permute-done((bf16[336,512]{1,0:T(8,128)(2,1)}, bf16[336,512]{1,0:T(8,128)(2,1)S(1)}, u32[]{:S(2)}, u32[]{:S(2)}) %collective-permute-start.5) | collective-permute-done | bytes 344096 | tf_op jit(solution)/shard_map/ppermute | solution.py:143
  90.1 6.2 collective-permute-done.6
  100.9 3.7 fusion.44
  116.3 21.3 %collective-permute-done.9 = bf16[2,512,512]{1,2,0:T(8,128)(2,1)S(1)} collective-permute-done((bf16[2,512,512]{1,2,0:T(8,128)(2,1)}, bf16[2,512,512]{1,2,0:T(8,128)(2,1)S(1)}, u32[]{:S(2)}, u32[]{:S(2)}) %collective-permute-start.9) | collective-permute-done | bytes 1048608 | tf_op jit(solution)/shard_map/ppermute | solution.py:55
  159.1 9.9 %collective-permute-done.11 = bf16[256,1152]{1,0:T(8,128)(2,1)S(1)} collective-permute-done((bf16[256,1152]{1,0:T(8,128)(2,1)S(1)}, bf16[256,1152]{1,0:T(8,128)(2,1)S(1)}, u32[]{:S(2)}, u32[]{:S(2)}) %collective-permute-start.11) | collective-permute-done | bytes 589856 | tf_op jit(solution)/shard_map/ppermute | solution.py:101
  173.8 29.3 %all-gather.11.cloned.1.call-done = bf16[576,1728]{1,0:T(8,128)(2,1)} async-done(((bf16[144,1728]{1,0:T(8,128)(2,1)}), bf16[576,1728]{1,0:T(8,128)(2,1)}) %all-gather.11.cloned.1.call-update) | async-done | bytes 1990672 | tf_op jit(solution)/shard_map/all_gather | solution.py:69
  206.3 43.0 %collective-permute-done.14 = bf16[4,144,1728]{2,1,0:T(8,128)(2,1)} collective-permute-done((bf16[4,144,1728]{2,1,0:T(8,128)(2,1)}, bf16[4,144,1728]{2,1,0:T(8,128)(2,1)}, u32[]{:S(2)}, u32[]{:S(2)}) %collective-permute-start.14) | collective-permute-done | bytes 1990688 | tf_op jit(solution)/shard_map/ppermute | solution.py:55
  253.1 39.2 %collective-permute-done.16 = bf16[4,144,1728]{2,1,0:T(8,128)(2,1)S(1)} collective-permute-done((bf16[4,144,1728]{2,1,0:T(8,128)(2,1)}, bf16[4,144,1728]{2,1,0:T(8,128)(2,1)S(1)}, u32[]{:S(2)}, u32[]{:S(2)}) %collective-permute-start.16) | collective-permute-done | bytes 1990688 | tf_op jit(solution)/shard_map/ppermute | solution.py:55
  293.5 7.2 fusion.121
  300.8 10.6 %multiply_convert_fusion.1 = (bf16[1024,1728]{0,1:T(8,128)(2,1)S(1)}, f32[1024,1728]{0,1:T(8,128)}) fusion(f32[1024,1728]{0,1:T(8,128)} %fusion.121, bf16[1024,1152]{1,0:T(8,128)(2,1)S(1)} %bitcast.372, bf16[1152,1728]{1,0:T(8,128)(2,1)S(1)} %bitcast.364), kind=kOutput, calls=%fused_computation.14 | convolution fusion | flops 4094558208 | bytes 24035328 | tf_op jit(solution)/shard_map/rd,df->rf/dot_general | solution.py:47
  311.4 5.3 convolution_convert_fusion.3
  322.8 13.8 %collective-permute-done.18 = bf16[256,1152]{1,0:T(8,128)(2,1)} collective-permute-done((bf16[256,1152]{1,0:T(8,128)(2,1)}, bf16[256,1152]{1,0:T(8,128)(2,1)}, u32[]{:S(2)}, u32[]{:S(2)}) %collective-permute-start.18) | collective-permute-done | bytes 589856 | tf_op jit(solution)/shard_map/ppermute | solution.py:101
  337.9 3.2 fusion.41
  343.3 14.1 %collective-permute-done.19 = bf16[256,1152]{1,0:T(8,128)(2,1)S(1)} collective-permute-done((bf16[256,1152]{1,0:T(8,128)(2,1)S(1)}, bf16[256,1152]{1,0:T(8,128)(2,1)S(1)}, u32[]{:S(2)}, u32[]{:S(2)}) %collective-permute-start.19) | collective-permute-done | bytes 589856 | tf_op jit(solution)/shard_map/ppermute | solution.py:101
  365.9 6.6 convolution_convert_fusion.2
  372.6 15.1 %multiply_convert_fusion = (bf16[1024,1728]{0,1:T(8,128)(2,1)}, bf16[1024,1728]{0,1:T(8,128)(2,1)}) fusion(f32[1024,1728]{0,1:T(8,128)} %fusion.121, f32[1024,1728]{0,1:T(8,128)} %get-tuple-element.138, bf16[1024,1152]{1,0:T(8,128)(2,1)S(1)} %bitcast.382, bf16[1152,1728]{1,0:T(8,128)(2,1)S(1)} %bitcast.369), kind=kOutput, calls=%fused_computation.13 | convolution fusion | flops 4119330816 | bytes 27574272 | tf_op jit(solution)/shard_map/rd,df->rf/dot_general | solution.py:47
  387.6 7.2 fusion.122
  394.8 5.5 add_convert_fusion
  402.4 6.5 copy.125
  408.8 3.2 dynamic-slice_bitcast_fusion
  413.5 9.2 %convolution_convert_fusion = bf16[1152,1728]{0,1:T(8,128)(2,1)} fusion(bf16[1024,1728]{0,1:T(8,128)(2,1)} %get-tuple-element.43, bf16[1024,1152]{1,0:T(8,128)(2,1)S(1)} %bitcast.373), kind=kOutput, calls=%fused_computation.3 | convolution fusion | flops 4078854144 | bytes 9879552 | tf_op jit(solution)/shard_map/rd,rf->df/dot_general | solution.py:47
  425.2 6.2 convolution_convert_fusion.1
  431.4 8.2 %collective-permute-done.22 = bf16[256,1152]{1,0:T(8,128)(2,1)S(1)} collective-permute-done((bf16[256,1152]{1,0:T(8,128)(2,1)S(1)}, bf16[256,1152]{1,0:T(8,128)(2,1)S(1)}, u32[]{:S(2)}, u32[]{:S(2)}) %collective-permute-start.22) | collective-permute-done | bytes 589856 | tf_op jit(solution)/shard_map/ppermute | solution.py:101
  447.1 6.4 copy.123
  453.6 5.6 collective-permute-done.46
  465.6 3.8 collective-permute-start.49
  472.3 6.7 copy.124
  479.0 3.0 dynamic-slice_bitcast_fusion.1
  483.8 10.3 %collective-permute-done.49 = bf16[144,1728]{1,0:T(8,128)(2,1)} collective-permute-done((bf16[144,1728]{1,0:T(8,128)(2,1)}, bf16[144,1728]{1,0:T(8,128)(2,1)}, u32[]{:S(2)}, u32[]{:S(2)}) %collective-permute-start.49) | collective-permute-done | bytes 497696 | tf_op jit(solution)/shard_map/ppermute | solution.py:80
  494.1 18.2 %collective-permute-done.48 = bf16[144,1728]{1,0:T(8,128)(2,1)} collective-permute-done((bf16[144,1728]{1,0:T(8,128)(2,1)}, bf16[144,1728]{1,0:T(8,128)(2,1)}, u32[]{:S(2)}, u32[]{:S(2)}) %collective-permute-start.48) | collective-permute-done | bytes 497696 | tf_op jit(solution)/shard_map/ppermute | solution.py:80
  530.8 3.8 convolution_convert_fusion.6
  545.3 3.8 collective-permute-start.41
  549.1 14.1 %collective-permute-done.42 = bf16[4,144,1728]{2,1,0:T(8,128)(2,1)} collective-permute-done((bf16[4,144,1728]{2,1,0:T(8,128)(2,1)}, bf16[4,144,1728]{2,1,0:T(8,128)(2,1)}, u32[]{:S(2)}, u32[]{:S(2)}) %collective-permute-start.42) | collective-permute-done | bytes 1990688 | tf_op jit(solution)/shard_map/ppermute | solution.py:55
  563.2 3.0 collective-permute-start.40
  571.1 3.8 collective-permute-start.45
  574.9 30.0 %collective-permute-done.40 = bf16[144,1728]{1,0:T(8,128)(2,1)S(1)} collective-permute-done((bf16[144,1728]{1,0:T(8,128)(2,1)S(1)}, bf16[144,1728]{1,0:T(8,128)(2,1)S(1)}, u32[]{:S(2)}, u32[]{:S(2)}) %collective-permute-start.40) | collective-permute-done | bytes 497696 | tf_op jit(solution)/shard_map/ppermute | solution.py:80
  606.1 29.7 %collective-permute-done.44 = bf16[144,1728]{1,0:T(8,128)(2,1)S(1)} collective-permute-done((bf16[144,1728]{1,0:T(8,128)(2,1)S(1)}, bf16[144,1728]{1,0:T(8,128)(2,1)S(1)}, u32[]{:S(2)}, u32[]{:S(2)}) %collective-permute-start.44) | collective-permute-done | bytes 497696 | tf_op jit(solution)/shard_map/ppermute | solution.py:80
  646.5 3.9 fusion.18
  673.7 3.0 collective-permute-done.33
  684.0 5.0 collective-permute-done.29
  697.8 3.6 collective-permute-done.34
  705.7 3.8 collective-permute-done.30
  710.0 3.8 collective-permute-start.37
  715.0 4.5 collective-permute-done.35
  721.5 9.0 %collective-permute-done.36 = bf16[192,512]{1,0:T(8,128)(2,1)S(1)} collective-permute-done((bf16[192,512]{1,0:T(8,128)(2,1)S(1)}, bf16[192,512]{1,0:T(8,128)(2,1)S(1)}, u32[]{:S(2)}, u32[]{:S(2)}) %collective-permute-start.36) | collective-permute-done | bytes 196640 | tf_op jit(solution)/shard_map/ppermute | solution.py:80
  (472 shorter events, 209.1 us)
Async XLA Ops:
  7.2 149.7 %all-gather.9.cloned.1.call-start = ((), (), s32[]{:S(2)}) async-start(), calls=%async_computation.1 | async-start | bytes 2580480 | tf_op jit(solution)/shard_map/all_gather | solution.py:69
  18.5 139.9 %all-gather.7.cloned.1.call-start = ((), (), s32[]{:S(2)}) async-start(), calls=%async_computation | async-start | bytes 2580480 | tf_op jit(solution)/shard_map/all_gather | solution.py:69
  21.5 34.8 %collective-permute-start.3 = (bf16[336,512]{1,0:T(8,128)(2,1)}, bf16[336,512]{1,0:T(8,128)(2,1)S(1)}, u32[]{:S(2)}, u32[]{:S(2)}) collective-permute-start(bf16[336,512]{1,0:T(8,128)(2,1)} %pad_maximum_fusion.23), channel_id=1, source_target_pairs={{0,8},{8,16},{16,24},{24,0},{1,9},{9,17},{17,25},{25,1},{2,10},{10... | collective-permute-start | bytes 1032200 | tf_op jit(solution)/shard_map/ppermute | solution.py:143
  23.6 31.2 %collective-permute-start.7 = (bf16[336,512]{1,0:T(8,128)(2,1)}, bf16[336,512]{1,0:T(8,128)(2,1)}, u32[]{:S(2)}, u32[]{:S(2)}) collective-permute-start(bf16[336,512]{1,0:T(8,128)(2,1)} %pad_maximum_fusion.23), channel_id=1, source_target_pairs={{0,24},{8,0},{16,8},{24,16},{1,25},{9,1},{17,9},{25,17},{2,26},{10... | collective-permute-start | bytes 1032200 | tf_op jit(solution)/shard_map/ppermute | solution.py:143
  25.6 60.8 %collective-permute-start.5 = (bf16[336,512]{1,0:T(8,128)(2,1)}, bf16[336,512]{1,0:T(8,128)(2,1)S(1)}, u32[]{:S(2)}, u32[]{:S(2)}) collective-permute-start(bf16[336,512]{1,0:T(8,128)(2,1)} %pad_maximum_fusion.23), channel_id=1, source_target_pairs={{0,16},{8,24},{16,0},{24,8},{1,17},{9,25},{17,1},{25,9},{2,18},{10... | collective-permute-start | bytes 1032200 | tf_op jit(solution)/shard_map/ppermute | solution.py:143
  26.6 61.3 %collective-permute-start.2 = (bf16[336,512]{1,0:T(8,128)(2,1)}, bf16[336,512]{1,0:T(8,128)(2,1)}, u32[]{:S(2)}, u32[]{:S(2)}) collective-permute-start(bf16[336,512]{1,0:T(8,128)(2,1)} %pad_maximum_fusion.23), channel_id=1, source_target_pairs={{0,4},{4,0},{1,5},{5,1},{2,6},{6,2},{3,7},{7,3},{8,12},{12,8},{9,1... | collective-permute-start | bytes 1032200 | tf_op jit(solution)/shard_map/ppermute | solution.py:55
  54.8 34.3 %collective-permute-start.8 = (bf16[336,512]{1,0:T(8,128)(2,1)}, bf16[336,512]{1,0:T(8,128)(2,1)S(1)}, u32[]{:S(2)}, u32[]{:S(2)}) collective-permute-start(bf16[336,512]{1,0:T(8,128)(2,1)} %collective-permute-done.7), channel_id=1, source_target_pairs={{0,4},{4,0},{1,5},{5,1},{2,6},{6,2},{3,7},{7,3},{8,12},{12,8},{9,1... | collective-permute-start | bytes 1032200 | tf_op jit(solution)/shard_map/ppermute | solution.py:55
  56.3 40.1 %collective-permute-start.4 = (bf16[336,512]{1,0:T(8,128)(2,1)S(1)}, bf16[336,512]{1,0:T(8,128)(2,1)S(1)}, u32[]{:S(2)}, u32[]{:S(2)}) collective-permute-start(bf16[336,512]{1,0:T(8,128)(2,1)S(1)} %collective-permute-done.3), channel_id=1, source_target_pairs={{0,4},{4,0},{1,5},{5,1},{2,6},{6,2},{3,7},{7,3},{8,12},{12,8},{9,1... | collective-permute-start | bytes 1032200 | tf_op jit(solution)/shard_map/ppermute | solution.py:55
  86.5 9.8 %collective-permute-start.6 = (bf16[336,512]{1,0:T(8,128)(2,1)S(1)}, bf16[336,512]{1,0:T(8,128)(2,1)S(1)}, u32[]{:S(2)}, u32[]{:S(2)}) collective-permute-start(bf16[336,512]{1,0:T(8,128)(2,1)S(1)} %collective-permute-done.5), channel_id=1, source_target_pairs={{0,4},{4,0},{1,5},{5,1},{2,6},{6,2},{3,7},{7,3},{8,12},{12,8},{9,1... | collective-permute-start | bytes 1032200 | tf_op jit(solution)/shard_map/ppermute | solution.py:55
  113.3 24.2 %collective-permute-start.9 = (bf16[2,512,512]{1,2,0:T(8,128)(2,1)}, bf16[2,512,512]{1,2,0:T(8,128)(2,1)S(1)}, u32[]{:S(2)}, u32[]{:S(2)}) collective-permute-start(bf16[2,512,512]{1,2,0:T(8,128)(2,1)} %pad_maximum_fusion.17), channel_id=1, source_target_pairs={{0,4},{4,0},{1,5},{5,1},{2,6},{6,2},{3,7},{7,3},{8,12},{12,8},{9,1... | collective-permute-start | bytes 3145736 | tf_op jit(solution)/shard_map/ppermute | solution.py:55
  114.9 88.2 %all-gather.11.cloned.1.call-start = ((), (), s32[]{:S(2)}) async-start(), calls=%async_computation.2 | async-start | bytes 2580480 | tf_op jit(solution)/shard_map/all_gather | solution.py:69
  153.6 15.4 %collective-permute-start.11 = (bf16[256,1152]{1,0:T(8,128)(2,1)S(1)}, bf16[256,1152]{1,0:T(8,128)(2,1)S(1)}, u32[]{:S(2)}, u32[]{:S(2)}) collective-permute-start(bf16[256,1152]{1,0:T(8,128)(2,1)S(1)} %dynamic-slice_bitcast_fusion.16), channel_id=1, source_target_pairs={{0,2},{1,3},{2,0},{3,1},{4,6},{5,7},{6,4},{7,5},{8,10},{9,11},{10,... | collective-permute-start | bytes 1769480 | tf_op jit(solution)/shard_map/ppermute | solution.py:101
  156.9 49.4 %collective-permute-start.15 = (bf16[4,144,1728]{2,1,0:T(8,128)(2,1)}, bf16[4,144,1728]{2,1,0:T(8,128)(2,1)}, u32[]{:S(2)}, u32[]{:S(2)}) collective-permute-start(bf16[4,144,1728]{2,1,0:T(8,128)(2,1)} %bitcast.383), channel_id=1, source_target_pairs={{0,4},{4,0},{1,5},{5,1},{2,6},{6,2},{3,7},{7,3},{8,12},{12,8},{9,1... | collective-permute-start | bytes 5971976 | tf_op jit(solution)/shard_map/ppermute | solution.py:55
  158.4 90.9 %collective-permute-start.14 = (bf16[4,144,1728]{2,1,0:T(8,128)(2,1)}, bf16[4,144,1728]{2,1,0:T(8,128)(2,1)}, u32[]{:S(2)}, u32[]{:S(2)}) collective-permute-start(bf16[4,144,1728]{2,1,0:T(8,128)(2,1)} %bitcast.385), channel_id=1, source_target_pairs={{0,4},{4,0},{1,5},{5,1},{2,6},{6,2},{3,7},{7,3},{8,12},{12,8},{9,1... | collective-permute-start | bytes 5971976 | tf_op jit(solution)/shard_map/ppermute | solution.py:55
  172.2 32.5 %collective-permute-start.12 = (bf16[256,1152]{1,0:T(8,128)(2,1)S(1)}, bf16[256,1152]{1,0:T(8,128)(2,1)}, u32[]{:S(2)}, u32[]{:S(2)}) collective-permute-start(bf16[256,1152]{1,0:T(8,128)(2,1)S(1)} %multiply_convert_fusion.4), channel_id=1, source_target_pairs={{0,2},{1,3},{2,0},{3,1},{4,6},{5,7},{6,4},{7,5},{8,10},{9,11},{10,... | collective-permute-start | bytes 1769480 | tf_op jit(solution)/shard_map/ppermute | solution.py:101
  203.1 89.2 %collective-permute-start.16 = (bf16[4,144,1728]{2,1,0:T(8,128)(2,1)}, bf16[4,144,1728]{2,1,0:T(8,128)(2,1)S(1)}, u32[]{:S(2)}, u32[]{:S(2)}) collective-permute-start(bf16[4,144,1728]{2,1,0:T(8,128)(2,1)} %bitcast.387), channel_id=1, source_target_pairs={{0,4},{4,0},{1,5},{5,1},{2,6},{6,2},{3,7},{7,3},{8,12},{12,8},{9,1... | collective-permute-start | bytes 5971976 | tf_op jit(solution)/shard_map/ppermute | solution.py:55
  206.2 86.8 %collective-permute-start.13 = (bf16[2,256,1152]{2,1,0:T(8,128)(2,1)S(1)}, bf16[2,256,1152]{2,1,0:T(8,128)(2,1)S(1)}, u32[]{:S(2)}, u32[]{:S(2)}) collective-permute-start(bf16[2,256,1152]{2,1,0:T(8,128)(2,1)S(1)} %pad_maximum_fusion.12), channel_id=1, source_target_pairs={{0,1},{1,0},{2,3},{3,2},{4,5},{5,4},{6,7},{7,6},{8,9},{9,8},{10,11... | collective-permute-start | bytes 3538952 | tf_op jit(solution)/shard_map/ppermute | solution.py:101
  320.9 15.7 %collective-permute-start.18 = (bf16[256,1152]{1,0:T(8,128)(2,1)}, bf16[256,1152]{1,0:T(8,128)(2,1)}, u32[]{:S(2)}, u32[]{:S(2)}) collective-permute-start(bf16[256,1152]{1,0:T(8,128)(2,1)} %dynamic-slice_bitcast_fusion.15), channel_id=1, source_target_pairs={{0,2},{1,3},{2,0},{3,1},{4,6},{5,7},{6,4},{7,5},{8,10},{9,11},{10,... | collective-permute-start | bytes 1769480 | tf_op jit(solution)/shard_map/ppermute | solution.py:101
  342.8 14.6 %collective-permute-start.19 = (bf16[256,1152]{1,0:T(8,128)(2,1)S(1)}, bf16[256,1152]{1,0:T(8,128)(2,1)S(1)}, u32[]{:S(2)}, u32[]{:S(2)}) collective-permute-start(bf16[256,1152]{1,0:T(8,128)(2,1)S(1)} %fusion.34), channel_id=1, source_target_pairs={{0,2},{1,3},{2,0},{3,1},{4,6},{5,7},{6,4},{7,5},{8,10},{9,11},{10,... | collective-permute-start | bytes 1769480 | tf_op jit(solution)/shard_map/ppermute | solution.py:101
  401.8 20.9 %collective-permute-start.21 = (bf16[2,256,1152]{2,1,0:T(8,128)(2,1)S(1)}, bf16[2,256,1152]{2,1,0:T(8,128)(2,1)}, u32[]{:S(2)}, u32[]{:S(2)}) collective-permute-start(bf16[2,256,1152]{2,1,0:T(8,128)(2,1)S(1)} %dynamic-slice_bitcast_fusion.4), channel_id=1, source_target_pairs={{0,1},{1,0},{2,3},{3,2},{4,5},{5,4},{6,7},{7,6},{8,9},{9,8},{10,11... | collective-permute-start | bytes 3538952 | tf_op jit(solution)/shard_map/ppermute | solution.py:101
  412.0 47.2 %collective-permute-start.46 = (bf16[4,144,1728]{2,1,0:T(8,128)(2,1)}, bf16[4,144,1728]{2,1,0:T(8,128)(2,1)}, u32[]{:S(2)}, u32[]{:S(2)}) collective-permute-start(bf16[4,144,1728]{2,1,0:T(8,128)(2,1)} %dynamic-slice_bitcast_fusion), channel_id=1, source_target_pairs={{0,4},{4,0},{1,5},{5,1},{2,6},{6,2},{3,7},{7,3},{8,12},{12,8},{9,1... | collective-permute-start | bytes 5971976 | tf_op jit(solution)/shard_map/ppermute | solution.py:55
  424.5 15.0 %collective-permute-start.22 = (bf16[256,1152]{1,0:T(8,128)(2,1)S(1)}, bf16[256,1152]{1,0:T(8,128)(2,1)S(1)}, u32[]{:S(2)}, u32[]{:S(2)}) collective-permute-start(bf16[256,1152]{1,0:T(8,128)(2,1)S(1)} %dynamic-slice_bitcast_fusion.14), channel_id=1, source_target_pairs={{0,2},{1,3},{2,0},{3,1},{4,6},{5,7},{6,4},{7,5},{8,10},{9,11},{10,... | collective-permute-start | bytes 1769480 | tf_op jit(solution)/shard_map/ppermute | solution.py:101
  444.4 17.4 %collective-permute-start.23 = (bf16[256,1152]{1,0:T(8,128)(2,1)}, bf16[256,1152]{1,0:T(8,128)(2,1)}, u32[]{:S(2)}, u32[]{:S(2)}) collective-permute-start(bf16[256,1152]{1,0:T(8,128)(2,1)} %multiply_convert_fusion.3), channel_id=1, source_target_pairs={{0,2},{1,3},{2,0},{3,1},{4,6},{5,7},{6,4},{7,5},{8,10},{9,11},{10,... | collective-permute-start | bytes 1769480 | tf_op jit(solution)/shard_map/ppermute | solution.py:101
  464.4 50.4 %collective-permute-start.24 = (bf16[2,256,1152]{2,1,0:T(8,128)(2,1)}, bf16[2,256,1152]{2,1,0:T(8,128)(2,1)}, u32[]{:S(2)}, u32[]{:S(2)}) collective-permute-start(bf16[2,256,1152]{2,1,0:T(8,128)(2,1)} %pad_maximum_fusion.14), channel_id=1, source_target_pairs={{0,1},{1,0},{2,3},{3,2},{4,5},{5,4},{6,7},{7,6},{8,9},{9,8},{10,11... | collective-permute-start | bytes 3538952 | tf_op jit(solution)/shard_map/ppermute | solution.py:101
  465.6 16.7 %collective-permute-start.47 = (bf16[144,1728]{1,0:T(8,128)(2,1)}, bf16[144,1728]{1,0:T(8,128)(2,1)}, u32[]{:S(2)}, u32[]{:S(2)}) collective-permute-start(bf16[144,1728]{1,0:T(8,128)(2,1)} %get-tuple-element.70), channel_id=1, source_target_pairs={{0,8},{8,16},{16,24},{24,0},{1,9},{9,17},{17,25},{25,1},{2,10},{10... | collective-permute-start | bytes 1493000 | tf_op jit(solution)/shard_map/ppermute | solution.py:80
  465.6 28.5 %collective-permute-start.49 = (bf16[144,1728]{1,0:T(8,128)(2,1)}, bf16[144,1728]{1,0:T(8,128)(2,1)}, u32[]{:S(2)}, u32[]{:S(2)}) collective-permute-start(bf16[144,1728]{1,0:T(8,128)(2,1)} %get-tuple-element.71), channel_id=1, source_target_pairs={{0,24},{8,0},{16,8},{24,16},{1,25},{9,1},{17,9},{25,17},{2,26},{10... | collective-permute-start | bytes 1493000 | tf_op jit(solution)/shard_map/ppermute | solution.py:80
  469.4 42.9 %collective-permute-start.48 = (bf16[144,1728]{1,0:T(8,128)(2,1)}, bf16[144,1728]{1,0:T(8,128)(2,1)}, u32[]{:S(2)}, u32[]{:S(2)}) collective-permute-start(bf16[144,1728]{1,0:T(8,128)(2,1)} %get-tuple-element.72), channel_id=1, source_target_pairs={{0,16},{8,24},{16,0},{24,8},{1,17},{9,25},{17,1},{25,9},{2,18},{10... | collective-permute-start | bytes 1493000 | tf_op jit(solution)/shard_map/ppermute | solution.py:80
  470.8 70.7 %collective-permute-start.38 = (bf16[4,144,1728]{2,1,0:T(8,128)(2,1)}, bf16[4,144,1728]{2,1,0:T(8,128)(2,1)}, u32[]{:S(2)}, u32[]{:S(2)}) collective-permute-start(bf16[4,144,1728]{2,1,0:T(8,128)(2,1)} %dynamic-slice_bitcast_fusion.2), channel_id=1, source_target_pairs={{0,4},{4,0},{1,5},{5,1},{2,6},{6,2},{3,7},{7,3},{8,12},{12,8},{9,1... | collective-permute-start | bytes 5971976 | tf_op jit(solution)/shard_map/ppermute | solution.py:55
  482.3 80.9 %collective-permute-start.42 = (bf16[4,144,1728]{2,1,0:T(8,128)(2,1)}, bf16[4,144,1728]{2,1,0:T(8,128)(2,1)}, u32[]{:S(2)}, u32[]{:S(2)}) collective-permute-start(bf16[4,144,1728]{2,1,0:T(8,128)(2,1)} %dynamic-slice_bitcast_fusion.1), channel_id=1, source_target_pairs={{0,4},{4,0},{1,5},{5,1},{2,6},{6,2},{3,7},{7,3},{8,12},{12,8},{9,1... | collective-permute-start | bytes 5971976 | tf_op jit(solution)/shard_map/ppermute | solution.py:55
  518.7 49.6 %collective-permute-start.25 = (bf16[256,1152]{1,0:T(8,128)(2,1)}, bf16[256,1152]{1,0:T(8,128)(2,1)}, u32[]{:S(2)}, u32[]{:S(2)}) collective-permute-start(bf16[256,1152]{1,0:T(8,128)(2,1)} %get-tuple-element.23), channel_id=1, source_target_pairs={{0,2},{1,3},{2,0},{3,1},{4,6},{5,7},{6,4},{7,5},{8,10},{9,11},{10,... | collective-permute-start | bytes 1769480 | tf_op jit(solution)/shard_map/ppermute | solution.py:101
  536.3 100.8 %collective-permute-start.27 = (bf16[2,512,512]{1,2,0:T(8,128)(2,1)S(1)}, bf16[2,512,512]{1,2,0:T(8,128)(2,1)S(1)}, u32[]{:S(2)}, u32[]{:S(2)}) collective-permute-start(bf16[2,512,512]{1,2,0:T(8,128)(2,1)S(1)} %fusion.50), channel_id=1, source_target_pairs={{0,4},{4,0},{1,5},{5,1},{2,6},{6,2},{3,7},{7,3},{8,12},{12,8},{9,1... | collective-permute-start | bytes 3145736 | tf_op jit(solution)/shard_map/ppermute | solution.py:55
  545.3 25.8 %collective-permute-start.39 = (bf16[144,1728]{1,0:T(8,128)(2,1)S(1)}, bf16[144,1728]{1,0:T(8,128)(2,1)S(1)}, u32[]{:S(2)}, u32[]{:S(2)}) collective-permute-start(bf16[144,1728]{1,0:T(8,128)(2,1)S(1)} %get-tuple-element.76), channel_id=1, source_target_pairs={{0,8},{8,16},{16,24},{24,0},{1,9},{9,17},{17,25},{25,1},{2,10},{10... | collective-permute-start | bytes 1493000 | tf_op jit(solution)/shard_map/ppermute | solution.py:80
  545.3 29.6 %collective-permute-start.41 = (bf16[144,1728]{1,0:T(8,128)(2,1)S(1)}, bf16[144,1728]{1,0:T(8,128)(2,1)S(1)}, u32[]{:S(2)}, u32[]{:S(2)}) collective-permute-start(bf16[144,1728]{1,0:T(8,128)(2,1)S(1)} %get-tuple-element.77), channel_id=1, source_target_pairs={{0,24},{8,0},{16,8},{24,16},{1,25},{9,1},{17,9},{25,17},{2,26},{10... | collective-permute-start | bytes 1493000 | tf_op jit(solution)/shard_map/ppermute | solution.py:80
  563.2 41.7 %collective-permute-start.40 = (bf16[144,1728]{1,0:T(8,128)(2,1)S(1)}, bf16[144,1728]{1,0:T(8,128)(2,1)S(1)}, u32[]{:S(2)}, u32[]{:S(2)}) collective-permute-start(bf16[144,1728]{1,0:T(8,128)(2,1)S(1)} %get-tuple-element.78), channel_id=1, source_target_pairs={{0,16},{8,24},{16,0},{24,8},{1,17},{9,25},{17,1},{25,9},{2,18},{10... | collective-permute-start | bytes 1493000 | tf_op jit(solution)/shard_map/ppermute | solution.py:80
  568.4 37.7 %collective-permute-start.43 = (bf16[144,1728]{1,0:T(8,128)(2,1)S(1)}, bf16[144,1728]{1,0:T(8,128)(2,1)S(1)}, u32[]{:S(2)}, u32[]{:S(2)}) collective-permute-start(bf16[144,1728]{1,0:T(8,128)(2,1)S(1)} %get-tuple-element.73), channel_id=1, source_target_pairs={{0,8},{8,16},{16,24},{24,0},{1,9},{9,17},{17,25},{25,1},{2,10},{10... | collective-permute-start | bytes 1493000 | tf_op jit(solution)/shard_map/ppermute | solution.py:80
  571.1 35.0 %collective-permute-start.45 = (bf16[144,1728]{1,0:T(8,128)(2,1)S(1)}, bf16[144,1728]{1,0:T(8,128)(2,1)S(1)}, u32[]{:S(2)}, u32[]{:S(2)}) collective-permute-start(bf16[144,1728]{1,0:T(8,128)(2,1)S(1)} %get-tuple-element.74), channel_id=1, source_target_pairs={{0,24},{8,0},{16,8},{24,16},{1,25},{9,1},{17,9},{25,17},{2,26},{10... | collective-permute-start | bytes 1493000 | tf_op jit(solution)/shard_map/ppermute | solution.py:80
  574.9 60.9 %collective-permute-start.44 = (bf16[144,1728]{1,0:T(8,128)(2,1)S(1)}, bf16[144,1728]{1,0:T(8,128)(2,1)S(1)}, u32[]{:S(2)}, u32[]{:S(2)}) collective-permute-start(bf16[144,1728]{1,0:T(8,128)(2,1)S(1)} %get-tuple-element.75), channel_id=1, source_target_pairs={{0,16},{8,24},{16,0},{24,8},{1,17},{9,25},{17,1},{25,9},{2,18},{10... | collective-permute-start | bytes 1493000 | tf_op jit(solution)/shard_map/ppermute | solution.py:80
  604.9 62.8 %collective-permute-start.26 = (bf16[2,256,1152]{2,1,0:T(8,128)(2,1)}, bf16[2,256,1152]{2,1,0:T(8,128)(2,1)}, u32[]{:S(2)}, u32[]{:S(2)}) collective-permute-start(bf16[2,256,1152]{2,1,0:T(8,128)(2,1)} %pad_maximum_fusion.15), channel_id=1, source_target_pairs={{0,1},{1,0},{2,3},{3,2},{4,5},{5,4},{6,7},{7,6},{8,9},{9,8},{10,11... | collective-permute-start | bytes 3538952 | tf_op jit(solution)/shard_map/ppermute | solution.py:101
  667.0 9.8 %collective-permute-start.33 = (bf16[288,512]{1,0:T(8,128)(2,1)S(1)}, bf16[288,512]{1,0:T(8,128)(2,1)S(1)}, u32[]{:S(2)}, u32[]{:S(2)}) collective-permute-start(bf16[288,512]{1,0:T(8,128)(2,1)S(1)} %dynamic-slice_bitcast_fusion.26), channel_id=1, source_target_pairs={{0,2},{1,3},{2,0},{3,1},{4,6},{5,7},{6,4},{7,5},{8,10},{9,11},{10,... | collective-permute-start | bytes 884744 | tf_op jit(solution)/shard_map/ppermute | solution.py:101
  672.6 16.3 %collective-permute-start.29 = (bf16[256,1152]{1,0:T(8,128)(2,1)}, bf16[256,1152]{1,0:T(8,128)(2,1)S(1)}, u32[]{:S(2)}, u32[]{:S(2)}) collective-permute-start(bf16[256,1152]{1,0:T(8,128)(2,1)} %dynamic-slice_bitcast_fusion.13), channel_id=1, source_target_pairs={{0,2},{1,3},{2,0},{3,1},{4,6},{5,7},{6,4},{7,5},{8,10},{9,11},{10,... | collective-permute-start | bytes 1769480 | tf_op jit(solution)/shard_map/ppermute | solution.py:101
  682.4 18.9 %collective-permute-start.34 = (bf16[4,192,512]{2,1,0:T(8,128)(2,1)}, bf16[4,192,512]{2,1,0:T(8,128)(2,1)}, u32[]{:S(2)}, u32[]{:S(2)}) collective-permute-start(bf16[4,192,512]{2,1,0:T(8,128)(2,1)} %dynamic-slice_bitcast_fusion.7), channel_id=1, source_target_pairs={{0,4},{4,0},{1,5},{5,1},{2,6},{6,2},{3,7},{7,3},{8,12},{12,8},{9,1... | collective-permute-start | bytes 2359304 | tf_op jit(solution)/shard_map/ppermute | solution.py:55
  694.3 15.2 %collective-permute-start.30 = (bf16[256,1152]{1,0:T(8,128)(2,1)S(1)}, bf16[256,1152]{1,0:T(8,128)(2,1)S(1)}, u32[]{:S(2)}, u32[]{:S(2)}) collective-permute-start(bf16[256,1152]{1,0:T(8,128)(2,1)S(1)} %fusion.39), channel_id=1, source_target_pairs={{0,2},{1,3},{2,0},{3,1},{4,6},{5,7},{6,4},{7,5},{8,10},{9,11},{10,... | collective-permute-start | bytes 1769480 | tf_op jit(solution)/shard_map/ppermute | solution.py:101
  705.1 8.7 %collective-permute-start.53 = (f32[160]{0:T(256)S(1)}, f32[160]{0:T(256)S(1)}, u32[]{:S(2)}, u32[]{:S(2)}) collective-permute-start(f32[160]{0:T(256)S(1)} %bitcast.407), channel_id=1, source_target_pairs={{0,8},{8,16},{16,24},{24,0},{1,9},{9,17},{17,25},{25,1},{2,10},{10... | collective-permute-start | bytes 1928 | tf_op jit(solution)/shard_map/ppermute | solution.py:80
  705.1 8.7 %collective-permute-start.54 = (f32[160]{0:T(256)S(1)}, f32[160]{0:T(256)S(1)}, u32[]{:S(2)}, u32[]{:S(2)}) collective-permute-start(f32[160]{0:T(256)S(1)} %bitcast.406), channel_id=1, source_target_pairs={{0,16},{8,24},{16,0},{24,8},{1,17},{9,25},{17,1},{25,9},{2,18},{10... | collective-permute-start | bytes 1928 | tf_op jit(solution)/shard_map/ppermute | solution.py:80
  709.7 22.3 %collective-permute-start.31 = (bf16[2,256,1152]{2,1,0:T(8,128)(2,1)S(1)}, bf16[2,256,1152]{2,1,0:T(8,128)(2,1)S(1)}, u32[]{:S(2)}, u32[]{:S(2)}) collective-permute-start(bf16[2,256,1152]{2,1,0:T(8,128)(2,1)S(1)} %pad_maximum_fusion.16), channel_id=1, source_target_pairs={{0,1},{1,0},{2,3},{3,2},{4,5},{5,4},{6,7},{7,6},{8,9},{9,8},{10,11... | collective-permute-start | bytes 3538952 | tf_op jit(solution)/shard_map/ppermute | solution.py:101
  709.9 9.6 %collective-permute-start.35 = (bf16[192,512]{1,0:T(8,128)(2,1)S(1)}, bf16[192,512]{1,0:T(8,128)(2,1)S(1)}, u32[]{:S(2)}, u32[]{:S(2)}) collective-permute-start(bf16[192,512]{1,0:T(8,128)(2,1)S(1)} %get-tuple-element.96), channel_id=1, source_target_pairs={{0,8},{8,16},{16,24},{24,0},{1,9},{9,17},{17,25},{25,1},{2,10},{10... | collective-permute-start | bytes 589832 | tf_op jit(solution)/shard_map/ppermute | solution.py:80
  710.0 11.6 %collective-permute-start.37 = (bf16[192,512]{1,0:T(8,128)(2,1)S(1)}, bf16[192,512]{1,0:T(8,128)(2,1)S(1)}, u32[]{:S(2)}, u32[]{:S(2)}) collective-permute-start(bf16[192,512]{1,0:T(8,128)(2,1)S(1)} %get-tuple-element.97), channel_id=1, source_target_pairs={{0,24},{8,0},{16,8},{24,16},{1,25},{9,1},{17,9},{25,17},{2,26},{10... | collective-permute-start | bytes 589832 | tf_op jit(solution)/shard_map/ppermute | solution.py:80
  713.8 16.8 %collective-permute-start.36 = (bf16[192,512]{1,0:T(8,128)(2,1)S(1)}, bf16[192,512]{1,0:T(8,128)(2,1)S(1)}, u32[]{:S(2)}, u32[]{:S(2)}) collective-permute-start(bf16[192,512]{1,0:T(8,128)(2,1)S(1)} %get-tuple-element.98), channel_id=1, source_target_pairs={{0,16},{8,24},{16,0},{24,8},{1,17},{9,25},{17,1},{25,9},{2,18},{10... | collective-permute-start | bytes 589832 | tf_op jit(solution)/shard_map/ppermute | solution.py:80
  (110 other events, 1222.8 us)
Sparse Core Ops, SparseCore 0:
  18.6 71.3 all-gather.8
  115.0 42.5 all-gather.6
  159.2 43.8 all-gather.10
